TPU v7x, 128 devices: a whole 4x4x4 slice. The times are simulated.
128 devices in a mesh: wide: 16 (over z_hi, y, core), narrow: 8 (over z_lo, x).
Axes of the slice: x: 4, y: 4, z: 4 (z_hi: 2, z_lo: 2; z = z_hi * 2 + z_lo), core: 2. Of those that a mesh axis runs over, the one named last changes fastest.
Arguments:
- tokens: bfloat16 [6144, 5120], P('wide'), may hold values from -6 to 6
- norm_gain: float32 [5120], replicated, may hold values from 0.1 to 1.9
- w_query: bfloat16 [5120, 5120], P('wide', 'narrow'), may hold values from -0.078125 to 0.078125
- w_keyval: bfloat16 [5120, 2, 1024], P('wide', None, 'narrow'), may hold values from -0.078125 to 0.078125
- w_output: bfloat16 [5120, 5120], P('narrow', 'wide'), may hold values from -0.75 to 0.75
- prompt_cache: bfloat16 [16, 2, 8192, 1024], P(None, None, 'wide', 'narrow'), may hold values from -64 to 64
- stretch_lengths: int32 [16], replicated, may hold values from 1 to 1536, 6144 in all
- stretch_starts: int32 [16], replicated, may hold values from 0 to 2047
- page_route: int32 [16, 16], P('wide'), may hold values from 0 to 15, each once within a row
Outputs:
- attn_out: bfloat16 [6144, 5120], P('wide', 'narrow')
- decode_layout_cache: bfloat16 [8, 8, 2, 256, 32, 256], P('narrow', None, None, 'wide')
Inputs may be any that keep to these rules, and one draw needn't show every extreme that they name: `stretch_lengths`: stretches sum to 6144 tokens; the longest has exactly 1536. `page_route`: each row is a permutation of 0 to 15.
All inputs are finite; a program needn't handle non-finite values.
Results may differ from a plain program's by a relative error of at most 0.017.
Values may be sent and summed in bfloat16 or wider, within the bound.
A program may use at most 128 MiB of HBM per device.

v0:
```python
import jax
import jax.numpy as jnp
from jax import lax
from jax.sharding import PartitionSpec as P

HEAD_SIZE = 128


def from_partner(value, axis, stride):
    mask = 2**stride
    pairs = [(source, source ^ mask) for source in range(lax.axis_size(axis))]
    return lax.ppermute(value, axis, pairs)


def rotate(heads, positions):
    half = heads.shape[-1] // 2
    freq = 1000000.0 ** (-jnp.arange(half, dtype=jnp.float32) * 2.0 / heads.shape[-1])
    angle = positions.astype(jnp.float32)[:, None] * freq[None, :]
    cosine = jnp.cos(angle)[:, None, :]
    sine = jnp.sin(angle)[:, None, :]
    first = heads[..., :half]
    second = heads[..., half:]
    return jnp.concatenate([first * cosine - second * sine, second * cosine + first * sine], -1)


def segment_of(tok_ids, ends):
    return jnp.sum((ends[None, :] <= tok_ids[:, None]).astype(jnp.int32), 1)


def relay_pages(prompt_cache, page_route):
    layers, kinds, cache_rows, channels = prompt_cache.shape
    per_block = page_route.shape[1]
    page_len = cache_rows // per_block
    pages = prompt_cache.reshape(layers, kinds, per_block, page_len, channels)
    inverse = (
        jnp.zeros((per_block,), jnp.int32)
        .at[page_route[0]]
        .set(jnp.arange(per_block, dtype=jnp.int32))
    )
    ordered = jnp.take(pages, inverse, axis=2)[:, :, :, None]
    moved = lax.all_to_all(ordered, "wide", split_axis=2, concat_axis=3, tiled=True)
    moved = moved.reshape(layers, kinds, per_block, page_len, channels)
    parity = lax.axis_index("narrow") % 2
    half = layers // 2
    keep = lax.dynamic_slice_in_dim(moved, parity * half, half, 0)
    outgoing = lax.dynamic_slice_in_dim(moved, (1 - parity) * half, half, 0)
    partner = from_partner(outgoing, "narrow", 0)
    joined = jnp.where(
        parity == 0, jnp.concatenate([keep, partner], -1), jnp.concatenate([partner, keep], -1)
    )
    return joined[None]


def on_device(
    tokens,
    norm_gain,
    w_query,
    w_keyval,
    w_output,
    prompt_cache,
    stretch_lengths,
    stretch_starts,
    page_route,
):
    decode_layout_cache = relay_pages(prompt_cache, page_route)
    tok_rows = tokens.shape[0]
    cache_rows = prompt_cache.shape[2]
    channels = prompt_cache.shape[3]
    head_dim = HEAD_SIZE
    kv_local = channels // head_dim
    q_cols = w_query.shape[1]
    q_local = q_cols // head_dim
    group = q_local // kv_local
    xfull = tokens.astype(jnp.float32)
    normed = (
        xfull * lax.rsqrt(jnp.mean(xfull * xfull, -1, keepdims=True) + 1e-06) * norm_gain
    ).astype(jnp.bfloat16)
    piece_q = lax.all_gather(w_query, "wide", axis=0, tiled=True)
    piece_kv = lax.all_gather(w_keyval, "wide", axis=0, tiled=True)
    rows = piece_q.shape[0]
    query = jnp.dot(normed, piece_q, preferred_element_type=jnp.float32)
    keyval = jnp.dot(
        normed, piece_kv.reshape(rows, 2 * channels), preferred_element_type=jnp.float32
    )
    keyval = keyval.reshape(tok_rows, 2, kv_local, head_dim)
    ends = jnp.cumsum(stretch_lengths)
    begins = ends - stretch_lengths
    tok_ids = lax.axis_index("wide") * tok_rows + jnp.arange(tok_rows, dtype=jnp.int32)
    seg = segment_of(tok_ids, ends)
    prompt_len = cache_rows * lax.axis_size("wide")
    onehot = (
        seg[:, None] == jnp.arange(stretch_lengths.shape[0], dtype=jnp.int32)[None, :]
    ).astype(jnp.int32)
    pos = prompt_len + jnp.sum(onehot * (stretch_starts - begins)[None, :], 1) + tok_ids
    rq = rotate(query.reshape(tok_rows, q_local, head_dim), pos).astype(jnp.bfloat16)
    rk = rotate(keyval[:, 0], pos).astype(jnp.bfloat16)
    rv = keyval[:, 1].astype(jnp.bfloat16)
    newblock = jnp.stack([rk.reshape(tok_rows, channels), rv.reshape(tok_rows, channels)], 0)
    keyblock = jnp.concatenate([prompt_cache[0], newblock], 1)
    span = cache_rows + tok_rows
    qgroup = rq.reshape(tok_rows, kv_local, group, head_dim)
    scale = head_dim ** (-0.5)

    def attend_block(carry, piece, start):
        top, den, acc = carry
        rows = piece.shape[1]
        index = start + jnp.arange(rows, dtype=jnp.int32)
        owner = index // span
        local = index % span
        is_prompt = local < cache_rows
        key_tok = owner * tok_rows + local - cache_rows
        key_seg = segment_of(key_tok, ends)
        keys = piece[0].reshape(rows, kv_local, head_dim)
        vals = piece[1].reshape(rows, kv_local, head_dim)
        score = (
            jnp.einsum("tkgd,skd->kgts", qgroup, keys, preferred_element_type=jnp.float32) * scale
        )
        visible = is_prompt[None, :] | (key_seg[None, :] == seg[:, None]) & (
            key_tok[None, :] <= tok_ids[:, None]
        )
        score = jnp.where(visible, score, -1e30)
        new_top = jnp.maximum(top, jnp.max(score, -1))
        factor = jnp.exp(top - new_top)
        weights = jnp.where(visible, jnp.exp(score - new_top[..., None]), 0.0)
        den = den * factor + jnp.sum(weights, -1)
        acc = acc * factor[..., None] + jnp.einsum(
            "kgts,skd->kgtd", weights.astype(jnp.bfloat16), vals, preferred_element_type=jnp.float32
        )
        return (new_top, den, acc)

    start_state = (
        jnp.full((kv_local, group, tok_rows), -1e30, jnp.float32),
        jnp.zeros((kv_local, group, tok_rows), jnp.float32),
        jnp.zeros((kv_local, group, tok_rows, head_dim), jnp.float32),
    )
    carry = start_state
    piece = lax.all_gather(keyblock, "wide", axis=1, tiled=True)
    rows = piece.shape[1]
    count = rows // span
    parts = jnp.transpose(piece.reshape(2, count, span, channels), (1, 0, 2, 3))

    def step(inner, item):
        number, part_piece = item
        return (attend_block(inner, part_piece, number * span), None)

    carry, unused = lax.scan(step, carry, (jnp.arange(count, dtype=jnp.int32), parts))
    top, den, acc = carry
    attn = (
        jnp.transpose(acc / den[..., None], (2, 0, 1, 3))
        .reshape(tok_rows, q_cols)
        .astype(jnp.bfloat16)
    )
    partial_out = jnp.dot(
        attn,
        lax.all_gather(w_output, "wide", axis=1, tiled=True),
        preferred_element_type=jnp.float32,
    )
    attn_out = lax.psum_scatter(
        partial_out.astype(jnp.bfloat16), "narrow", scatter_dimension=1, tiled=True
    )
    return (attn_out, decode_layout_cache)


def solution(mesh):
    placed = (
        P("wide", None),
        P(),
        P("wide", "narrow"),
        P("wide", None, "narrow"),
        P("narrow", "wide"),
        P(None, None, "wide", "narrow"),
        P(),
        P(),
        P("wide", None),
    )
    return jax.shard_map(
        on_device,
        mesh=mesh,
        in_specs=placed,
        out_specs=(P("wide", "narrow"), P("narrow", None, None, "wide", None, None)),
        check_vma=False,
    )
```

profile of v0, /device:TPU:32, one launch (start us, length us, event | category | flops | bytes accessed | tf_op | source)
XLA Modules:
  0.0 614.7 jit_solution(10323567279533854637)
XLA Ops:
  14.4 47.6 %all-gather.5.cloned.1.call-done = bf16[5120,2,128]{2,1,0:T(2,128)(2,1)} async-done(((bf16[320,2,128]{2,1,0:T(2,128)(2,1)}), bf16[5120,2,128]{2,1,0:T(2,128)(2,1)}) %all-gather.5.cloned.1.call-update) | async-done | bytes 2621456 | tf_op jit(solution)/shard_map/all_gather | solution.py:79
  62.1 5.9 copy.64
  67.9 3.7 fusion.34
  74.3 54.2 %all-gather.9.cloned.1.call-done = bf16[5120,640]{1,0:T(8,128)(2,1)} async-done(((bf16[320,640]{1,0:T(8,128)(2,1)}), bf16[5120,640]{1,0:T(8,128)(2,1)}) %all-gather.9.cloned.1.call-update) | async-done | bytes 6553616 | tf_op jit(solution)/shard_map/all_gather | solution.py:78
  128.5 7.7 %fusion.37 = f32[384,640]{0,1:T(8,128)S(1)} fusion(bf16[5120,640]{1,0:T(8,128)(2,1)} %all-gather.9.cloned.1.call-done, bf16[384,5120]{1,0:T(8,128)(2,1)} %param.11, f32[5120]{0:T(1024)S(1)} %copy-done.1, f32[384]{0:T(512)S(1)} %add_rsqrt_fusion), kind=kOutput, calls=%fused_computation.57 | convolution fusion | flops 2524446720 | bytes 11490816 | tf_op jit(solution)/shard_map/dot_general | solution.py:81
  136.7 61.6 %all-gather.7.cloned.1.call-done = bf16[2,14336,128]{2,1,0:T(8,128)(2,1)} async-done(((bf16[2,896,128]{2,1,0:T(8,128)(2,1)}), bf16[2,14336,128]{2,1,0:T(8,128)(2,1)}) %all-gather.7.cloned.1.call-update) | async-done | bytes 7340048 | tf_op jit(solution)/shard_map/all_gather | solution.py:137
  198.4 241.2 %while.17 = (s32[]{:T(128)}, f32[1,5,384]{2,1,0:T(8,128)S(1)}, f32[1,5,384]{2,1,0:T(8,128)S(1)}, f32[1,5,384,128]{3,2,1,0:T(8,128)S(1)}, s32[16]{0:T(128)S(1)}, ...) while((s32[]{:T(128)}, f32[1,5,384]{2,1,0:T(8,128)S(1)}, ...), condition=%wide.region_8.9_spmd.clone, body=%wide.region_4.8_spmd.clone.sunk | while | flops 905357056 | bytes 53535764 | solution.py:146
  201.6 4.2 fusion.69
  205.8 4.8 fusion.71
  217.1 4.2 fusion.69
  221.3 4.8 fusion.71
  232.1 4.2 fusion.69
  236.3 4.8 fusion.71
  247.2 4.2 fusion.69
  251.4 4.9 fusion.71
  262.5 4.2 fusion.69
  266.7 4.8 fusion.71
  277.5 4.2 fusion.69
  281.7 4.8 fusion.71
  292.5 4.2 fusion.69
  296.7 4.8 fusion.71
  307.6 4.2 fusion.69
  311.8 4.8 fusion.71
  322.6 4.2 fusion.69
  326.8 4.8 fusion.71
  337.6 4.2 fusion.69
  341.8 4.8 fusion.71
  352.7 4.2 fusion.69
  356.9 4.8 fusion.71
  367.7 4.2 fusion.69
  371.9 4.8 fusion.71
  382.7 4.2 fusion.69
  386.9 4.8 fusion.71
  397.8 4.2 fusion.69
  402.0 4.8 fusion.71
  412.8 4.2 fusion.69
  417.0 4.8 fusion.71
  427.8 4.2 fusion.69
  432.0 4.8 fusion.71
  440.0 8.0 %convolution_convert_fusion = bf16[384,5120]{1,0:T(8,128)(2,1)} fusion(bf16[384,640]{0,1:T(8,128)(2,1)S(1)} %bitcast.153, bf16[640,5120]{0,1:T(8,128)(2,1)} %all-gather.11.cloned.1.call-done), kind=kOutput, calls=%fused_computation.48 | convolution fusion | flops 2518548480 | bytes 10977280 | tf_op jit(solution)/shard_map/dot_general | solution.py:153
  448.1 6.3 %copy.65 = bf16[384,5120]{0,1:T(8,128)(2,1)} copy(bf16[384,5120]{1,0:T(8,128)(2,1)} %convolution_convert_fusion) | data formatting | bytes 7864320
  455.1 5.3 gather_fusion
  460.4 5.0 fusion.33
  465.4 4.8 all-to-all-start
  470.2 77.9 %all-to-all-done = bf16[16,2,16,1,32,128]{5,4,1,0,3,2:T(8,128)(2,1)} async-done(((bf16[16,2,16,1,32,128]{5,4,1,0,3,2:T(8,128)(2,1)}), bf16[16,2,16,1,32,128]{5,4,1,0,3,2:T(8,128)(2,1)}, u32[]{:S(2)}, u32[]{:S(2)}) %all-to-all-start) | async-done | bytes 4194336 | tf_op jit(solution)/shard_map/all_to_all | solution.py:41
  548.1 3.3 constant_dynamic-slice_fusion.1
  553.6 47.5 %collective-permute-done = bf16[8,2,16,32,128]{4,3,2,1,0:T(8,128)(2,1)} collective-permute-done((bf16[8,2,16,32,128]{4,3,2,1,0:T(8,128)(2,1)}, bf16[8,2,16,32,128]{4,3,2,1,0:T(8,128)(2,1)}, u32[]{:S(2)}, u32[]{:S(2)}) %collective-permute-start) | collective-permute-done | bytes 2097184 | tf_op jit(solution)/shard_map/ppermute | solution.py:12
  601.1 5.0 maximum_select_fusion
  (262 shorter events, 101.8 us)
Async XLA Ops:
  7.2 54.9 %all-gather.5.cloned.1.call-start = ((), (), s32[]{:S(2)}) async-start(), calls=%async_computation.2 | async-start | bytes 2785280 | tf_op jit(solution)/shard_map/all_gather | solution.py:79
  7.9 120.6 %all-gather.9.cloned.1.call-start = ((), (), s32[]{:S(2)}) async-start(), calls=%async_computation.4 | async-start | bytes 6963200 | tf_op jit(solution)/shard_map/all_gather | solution.py:78
  8.6 189.7 %all-gather.7.cloned.1.call-start = ((), (), s32[]{:S(2)}) async-start(), calls=%async_computation.3 | async-start | bytes 7798784 | tf_op jit(solution)/shard_map/all_gather | solution.py:137
  10.5 57.5 %copy-start.1 = (f32[5120]{0:T(1024)S(1)}, f32[5120]{0:T(1024)}, u32[]{:S(2)}) copy-start(f32[5120]{0:T(1024)} %param.12) | copy-start | bytes 61444
  73.2 366.8 %all-gather.11.cloned.1.call-start = ((), (), s32[]{:S(2)}) async-start(), calls=%async_computation.5 | async-start | bytes 6963200 | tf_op jit(solution)/shard_map/all_gather | solution.py:155
  73.8 532.3 %reduce-scatter.4.cloned.1.call-start = ((), (), s32[]{:S(2)}) async-start(), calls=%async_computation.6 | async-start | bytes 4423680
  205.8 5.3 copy-start
  221.3 4.9 copy-start
  236.3 4.9 copy-start
  251.4 5.2 copy-start
  266.7 4.9 copy-start
  281.7 4.9 copy-start
  296.7 4.9 copy-start
  311.8 4.9 copy-start
  326.8 4.9 copy-start
  341.8 4.9 copy-start
  356.9 4.9 copy-start
  371.9 4.9 copy-start
  386.9 4.9 copy-start
  401.9 4.9 copy-start
  417.0 4.9 copy-start
  432.0 4.9 copy-start
  448.1 6.3 %copy-start.2 = (s32[1,16]{1,0:T(1,128)S(1)}, s32[1,16]{1,0:T(1,128)}, u32[]{:S(2)}) copy-start(s32[1,16]{1,0:T(1,128)} %param.19) | copy-start | bytes 196
  465.4 82.6 %all-to-all-start = ((bf16[16,2,16,1,32,128]{5,4,1,0,3,2:T(8,128)(2,1)}), bf16[16,2,16,1,32,128]{5,4,1,0,3,2:T(8,128)(2,1)}, u32[]{:S(2)}, u32[]{:S(2)}) async-start(bf16[16,2,16,1,32,128]{5,4,1,0,3,2:T(8,128)(2,1)} %fusion.33), calls=%async_computation | async-start | bytes 8388608 | tf_op jit(solution)/shard_map/all_to_all | solution.py:41
  553.1 48.0 %collective-permute-start = (bf16[8,2,16,32,128]{4,3,2,1,0:T(8,128)(2,1)}, bf16[8,2,16,32,128]{4,3,2,1,0:T(8,128)(2,1)}, u32[]{:S(2)}, u32[]{:S(2)}) collective-permute-start(bf16[8,2,16,32,128]{4,3,2,1,0:T(8,128)(2,1)} %bitcast.117), channel_id=1, source_target_pairs={{0,1},{1,0},{2,3},{3,2},{4,5},{5,4},{6,7},{7,6},{8,9},{9,8},{10,11... | collective-permute-start | bytes 6291464 | tf_op jit(solution)/shard_map/ppermute | solution.py:12
Sparse Core Ops, SparseCore 0:
  10.4 51.5 all-gather.4
  64.5 63.9 all-gather.8
  131.6 66.7 all-gather.6
  200.6 63.0 all-gather.10
  454.5 74.8 reduce-scatter.3
where the time goes:
time: 618 us; the launch traced here: 615 us
  waiting for transfers between devices  291 us (47%)
  matrix products  128 us (21%)
  other arithmetic  108 us (17%)
  local copies, waits for them, and re-layouts  56.5 us (9%)
  between operations  14 us (2%)
  loops' own time  11.5 us (2%)
    all_to_all x1, waiting for transfers between devices, relay_pages(): lax.all_to_all(ordered, 'wide', split_axis=2, concat_axis=3, tiled=True)  77.9 us
    reduce_sum x16, other arithmetic, attend_block(): den = den * factor + jnp.sum(weights, -1)  76.6 us
    dot_general x16, matrix products, attend_block(): jnp.einsum('tkgd,skd->kgts', qgroup, keys, preferred_element_type=jnp.flo...  66.8 us
    all_gather x1, waiting for transfers between devices, on_device(): piece = lax.all_gather(keyblock, 'wide', axis=1, tiled=True)  61.6 us
    all_gather x1, waiting for transfers between devices, on_device(): piece_q = lax.all_gather(w_query, 'wide', axis=0, tiled=True)  54.2 us
    all_gather x1, waiting for transfers between devices, on_device(): piece_kv = lax.all_gather(w_keyval, 'wide', axis=0, tiled=True)  47.6 us
    ppermute x1, waiting for transfers between devices, from_partner(): return lax.ppermute(value, axis, pairs)  47.5 us
    dot_general x16, matrix products, attend_block(): jnp.einsum('kgts,skd->kgtd', weights.astype(jnp.bfloat16), vals, preferre...  42.1 us
  transfers between devices with their start and end apart: 7, of which 5 were waited for; matrix products, arithmetic and copies ran while one was open for 45% of the time, Pallas kernels for 0%

commit v1 on v0

v1 whole, which is shorter than its diff:
```python
import functools

import jax
import jax.numpy as jnp
from jax import lax
from jax.experimental import pallas as pl
from jax.experimental.pallas import tpu as pltpu
from jax.sharding import PartitionSpec as P

MESH = pl.DeviceIdType.MESH
HEAD = 128
GROUP = 5
REQUESTS = 16
WIDE = 16
NARROW = 8
BF16 = jnp.bfloat16
F32 = jnp.float32
KEYS = 1024
BACK = 4
LOG2E = 1.4426950408889634
MESSAGES = 17


def whole_kernel(
    tok_hbm,
    gain_ref,
    wqkv_hbm,
    wo_hbm,
    cache_hbm,
    freq_ref,
    lengths_ref,
    starts_ref,
    route_ref,
    out_ref,
    relay_ref,
    x_v,
    wqkv_v,
    kvp_v,
    wot_v,
    wo_v,
    comb_v,
    stage_v,
    proj_v,
    q_v,
    nkv_v,
    att_v,
    acc_v,
    top_v,
    den_v,
    cos_v,
    sin_v,
    begin_v,
    out_v,
    local_sem,
    g_send,
    g_recv,
    t_send,
    t_recv,
    x_send,
    x_recv,
    r_send,
    r_recv,
    n_send,
    n_recv,
    a_send,
    a_recv,
):
    tok_rows, depth = x_v.shape
    rows = wqkv_hbm.shape[0]
    cols = wqkv_hbm.shape[1]
    page_rows = comb_v.shape[3]
    half_layers = comb_v.shape[0]
    w = lax.axis_index("wide")
    n = lax.axis_index("narrow")
    core = lax.rem(w, 2)
    y = lax.rem(w // 2, 4)
    zh = w // 8
    plane = zh * 8

    def at_y(step):
        return plane + lax.rem(y + step, 4) * 2 + core

    def sib(chunk):
        return chunk + 1 - 2 * core

    def over_z(chunk):
        return lax.rem(chunk + 8, 16)

    yr, yl, y2 = at_y(1), at_y(3), at_y(2)
    par = lax.rem(n, 2)
    partner = n + 1 - 2 * par
    twin_w, twin_n = 2 * n + core, w // 2
    has_twin = twin_n != n

    half_at = pl.multiple_of(par * HEAD, HEAD)
    copies = [
        pltpu.make_async_copy(tok_hbm, x_v, local_sem.at[0]),
        pltpu.make_async_copy(
            wqkv_hbm, wqkv_v.at[pl.ds(pl.multiple_of(w * rows, 64), rows)], local_sem.at[1]
        ),
        pltpu.make_async_copy(
            cache_hbm.at[pl.ds(par * half_layers, half_layers)],
            comb_v.at[:, :, :, :, pl.ds(half_at, HEAD)],
            local_sem.at[2],
        ),
        pltpu.make_async_copy(cache_hbm.at[0], kvp_v.at[w], local_sem.at[3]),
    ]
    for copy in copies:
        copy.start()

    barrier = pltpu.get_barrier_semaphore()

    def greet_wide(k, carry):
        pl.semaphore_signal(barrier, inc=1, device_id=(lax.rem(w + k, WIDE), n), device_id_type=MESH)
        return carry

    def greet_narrow(k, carry):
        pl.semaphore_signal(barrier, inc=1, device_id=(w, lax.rem(n + k, NARROW)), device_id_type=MESH)
        return carry

    lax.fori_loop(1, WIDE, greet_wide, 0)
    lax.fori_loop(1, NARROW, greet_narrow, 0)

    peers = WIDE - 1 + NARROW - 1

    @pl.when(has_twin)
    def _():
        pl.semaphore_signal(barrier, inc=1, device_id=(twin_w, twin_n), device_id_type=MESH)
        pl.semaphore_wait(barrier, peers + 1)

    @pl.when(jnp.logical_not(has_twin))
    def _():
        pl.semaphore_wait(barrier, peers)

    def twin_copy():
        return pltpu.make_async_remote_copy(
            src_ref=wo_hbm, dst_ref=wot_v, send_sem=t_send, recv_sem=t_recv,
            device_id=(twin_w, twin_n), device_id_type=MESH,
        )

    own_wo = pltpu.make_async_copy(wo_hbm, wot_v, local_sem.at[4])

    @pl.when(has_twin)
    def _():
        twin_copy().start()

    @pl.when(jnp.logical_not(has_twin))
    def _():
        own_wo.start()

    def row_view(ref):
        def view(chunk, part=None):
            first = pl.multiple_of(chunk * rows, 64)
            if part is None:
                return ref.at[pl.ds(first, rows)]
            return ref.at[pl.ds(pl.multiple_of(first + part * (rows // 2), 32), rows // 2)]

        return view

    def prompt_view(chunk, part=None):
        return kvp_v.at[chunk] if part is None else kvp_v.at[chunk, part]

    views = [row_view(wqkv_v), prompt_view, row_view(wo_v)]
    owns = [wqkv_hbm, cache_hbm.at[0], wot_v]
    started = []

    def message(a, kind, chunk, part, to, own=False):
        dst = views[a](chunk, part)
        return pltpu.make_async_remote_copy(
            src_ref=owns[a] if own else dst,
            dst_ref=dst,
            send_sem=g_send.at[a, kind],
            recv_sem=g_recv.at[a, kind],
            device_id=(to, n),
            device_id_type=MESH,
        )

    def send(a, kind, chunk, part, to, own=False):
        copy = message(a, kind, chunk, part, to, own)
        copy.start()
        started.append(copy)

    def arrived(a, kind, chunk, part=None):
        message(a, kind, chunk, part, w).wait_recv()

    def first(a):
        send(a, 1, w, None, over_z(w), True)
        send(a, 2, w, None, yr, True)
        send(a, 3, w, None, yl, True)
        send(a, 0, w, None, sib(w), True)

    def second(a):
        chunk = over_z(w)
        arrived(a, 1, chunk)
        send(a, 5, chunk, None, yr)
        send(a, 6, chunk, None, yl)
        send(a, 4, chunk, None, sib(w))

    def third(a):
        arrived(a, 2, yl)
        send(a, 8, yl, 0, yr)
        send(a, 7, yl, None, sib(w))
        arrived(a, 3, yr)
        send(a, 10, yr, 1, yl)
        send(a, 9, yr, None, sib(w))

    def fourth(a):
        left, right = over_z(yl), over_z(yr)
        arrived(a, 5, left)
        send(a, 12, left, 0, yr)
        send(a, 11, left, None, sib(w))
        arrived(a, 6, right)
        send(a, 14, right, 1, yl)
        send(a, 13, right, None, sib(w))

    def fifth(a):
        arrived(a, 8, y2, 0)
        arrived(a, 10, y2, 1)
        send(a, 15, y2, None, sib(w))
        far = over_z(y2)
        arrived(a, 12, far, 0)
        arrived(a, 14, far, 1)
        send(a, 16, far, None, sib(w))

    def finish(a):
        for kind, chunk in (
            (0, w), (4, over_z(w)), (7, yl), (9, yr),
            (11, over_z(yl)), (13, over_z(yr)), (15, y2), (16, over_z(y2)),
        ):
            arrived(a, kind, sib(chunk))

    exchange = pltpu.make_async_remote_copy(
        src_ref=cache_hbm.at[pl.ds((1 - par) * half_layers, half_layers)],
        dst_ref=comb_v.at[:, :, :, :, pl.ds(half_at, HEAD)],
        send_sem=x_send, recv_sem=x_recv, device_id=(w, partner), device_id_type=MESH,
    )
    first(0)
    first(1)
    exchange.start()

    tok_id = w * tok_rows + lax.broadcasted_iota(jnp.int32, (tok_rows, HEAD), 0)
    begin = jnp.zeros((tok_rows, HEAD), jnp.int32)
    off = jnp.zeros((tok_rows, HEAD), jnp.int32)
    edge = jnp.int32(0)
    for k in range(REQUESTS):
        inside = tok_id >= edge
        begin = jnp.where(inside, edge, begin)
        off = jnp.where(inside, starts_ref[k] - edge, off)
        edge = edge + lengths_ref[k]
    begin_v[...] = begin
    block_keys = kvp_v.shape[2] * kvp_v.shape[3]
    prompt_len = WIDE * block_keys
    angle = (prompt_len + off + tok_id).astype(F32) * freq_ref[...]
    cos_v[...] = jnp.cos(angle)
    lane = lax.broadcasted_iota(jnp.int32, (tok_rows, HEAD), 1)
    sin_v[...] = jnp.where(lane < HEAD // 2, -1.0, 1.0) * jnp.sin(angle)

    copies[0].wait()
    block = 32

    def norm_block(i, carry):
        at = pl.ds(pl.multiple_of(i * block, block), block)
        xf = x_v[at, :].astype(F32)
        mean = jnp.sum(xf * xf, -1, keepdims=True) * (1.0 / depth)
        x_v[at, :] = (xf * lax.rsqrt(mean + 1e-06) * gain_ref[...]).astype(BF16)
        return carry

    lax.fori_loop(0, tok_rows // block, norm_block, 0)

    second(0)
    third(0)

    @pl.when(has_twin)
    def _():
        twin_copy().wait_recv()

    @pl.when(jnp.logical_not(has_twin))
    def _():
        own_wo.wait()

    first(2)
    own_wo2 = pltpu.make_async_copy(wot_v, views[2](w), local_sem.at[5])
    own_wo2.start()
    second(1)
    fourth(0)
    third(1)
    second(2)
    fifth(0)
    third(2)
    finish(0)
    copies[1].wait()

    proj_v[...] = jnp.zeros_like(proj_v)
    step = 1280

    def project(i, carry):
        at = pl.ds(pl.multiple_of(i * step, step), step)
        proj_v[...] += jnp.dot(x_v[:, at], wqkv_v[at, :], preferred_element_type=F32)
        return carry

    lax.fori_loop(0, depth // step, project, 0)

    def rotated(heads):
        return (heads * cos_v[...] + pltpu.roll(heads, HEAD // 2, 1) * sin_v[...]).astype(BF16)

    nkv_v[0, 0] = rotated(proj_v[:, GROUP * HEAD : (GROUP + 1) * HEAD])
    nkv_v[0, 1] = proj_v[:, (GROUP + 1) * HEAD : (GROUP + 2) * HEAD].astype(BF16)
    back_copies = []
    for j in range(1, BACK + 1):
        copy = pltpu.make_async_remote_copy(
            src_ref=nkv_v.at[0], dst_ref=nkv_v.at[j],
            send_sem=n_send.at[j], recv_sem=n_recv.at[j],
            device_id=(lax.rem(w + j, WIDE), n), device_id_type=MESH,
        )
        copy.start()
        back_copies.append(copy)
    for h in range(GROUP):
        q_v[h] = rotated(proj_v[:, h * HEAD : (h + 1) * HEAD])

    fourth(1)
    fifth(1)
    fourth(2)
    fifth(2)

    copies[2].wait()
    exchange.wait_recv()

    def relay_copy(k, to, source):
        return pltpu.make_async_remote_copy(
            src_ref=stage_v.at[to], dst_ref=relay_ref.at[0, :, :, source],
            send_sem=r_send.at[k], recv_sem=r_recv.at[k],
            device_id=(to, n), device_id_type=MESH,
        )

    def lay_out(k):
        to = lax.rem(w + k, WIDE)
        page = jnp.int32(0)
        for t in range(WIDE):
            page = jnp.where(route_ref[0, t] == to, jnp.int32(t), page)
        stage_v[to] = comb_v[:, :, page]
        return to

    def relay_step(k, carry):
        to = lay_out(k)
        relay_copy(k, to, w).start()
        return carry

    lax.fori_loop(1, WIDE, relay_step, 0)
    lay_out(0)
    own_page = pltpu.make_async_copy(stage_v.at[w], relay_ref.at[0, :, :, w], local_sem.at[6])
    own_page.start()

    finish(1)
    copies[3].wait()
    for copy in back_copies:
        copy.wait()

    factor = HEAD ** (-0.5) * LOG2E

    def attend(h, keys, vals, visible):
        score = lax.dot_general(
            q_v[h], keys, (((1,), (1,)), ((), ())), preferred_element_type=F32
        ) * factor
        if visible is not None:
            score = jnp.where(visible, score, -1e30)
        top = top_v[...]
        new_top = jnp.maximum(top, jnp.max(score, 1, keepdims=True))
        fall = jnp.exp2(top - new_top)
        weight = jnp.exp2(score - new_top[:, :1])
        part = weight[:, :HEAD]
        for i in range(1, weight.shape[1] // HEAD):
            part = part + weight[:, i * HEAD : (i + 1) * HEAD]
        den_v[...] = den_v[...] * fall + part
        acc_v[...] = acc_v[...] * fall + jnp.dot(
            weight.astype(BF16), vals, preferred_element_type=F32
        )
        top_v[...] = new_top

    per_step = KEYS // block_keys
    ring = (n // 4) * 4
    across = lax.rem(n + 4, NARROW)

    def around(k):
        return ring + lax.rem(n + k, 4)

    def head_copy(h, kind, owner, to):
        at = att_v.at[owner, :, pl.ds(pl.multiple_of(h * HEAD, HEAD), HEAD)]
        return pltpu.make_async_remote_copy(
            src_ref=at, dst_ref=at, send_sem=a_send.at[h, kind], recv_sem=a_recv.at[h, kind],
            device_id=(w, to), device_id_type=MESH,
        )

    def forward(h):
        head_copy(h, 3, across, n).wait_recv()
        head_copy(h, 4, across, around(1)).start()
        head_copy(h, 5, across, around(2)).start()
        head_copy(h, 6, across, around(3)).start()

    def head_step(h, carry):
        top_v[...] = jnp.full_like(top_v, -1e30)
        den_v[...] = jnp.zeros_like(den_v)
        acc_v[...] = jnp.zeros_like(acc_v)

        def prompt_step(i, inner):
            at = pl.ds(i * per_step, per_step)
            attend(h, kvp_v[at, 0].reshape(KEYS, HEAD), kvp_v[at, 1].reshape(KEYS, HEAD), None)
            return inner

        lax.fori_loop(0, WIDE // per_step, prompt_step, 0)

        def new_step(j, inner):
            key_id = (w - j) * tok_rows + lax.broadcasted_iota(jnp.int32, (tok_rows, tok_rows), 1)
            own_id = w * tok_rows + lax.broadcasted_iota(jnp.int32, (tok_rows, tok_rows), 0)
            visible = (key_id >= begin_v[:, :1]) & (key_id <= own_id)
            attend(h, nkv_v[j, 0], nkv_v[j, 1], visible)
            return inner

        lax.fori_loop(0, BACK + 1, new_step, 0)
        den = jnp.sum(den_v[...], 1, keepdims=True)
        att_v[n, :, pl.ds(pl.multiple_of(h * HEAD, HEAD), HEAD)] = (acc_v[...] / den).astype(BF16)
        head_copy(h, 3, n, across).start()
        head_copy(h, 0, n, around(1)).start()
        head_copy(h, 1, n, around(2)).start()
        head_copy(h, 2, n, around(3)).start()

        @pl.when(h > 0)
        def _():
            forward(h - 1)

        return carry

    lax.fori_loop(0, GROUP, head_step, 0)
    forward(GROUP - 1)

    finish(2)
    own_wo2.wait()
    out_v[...] = jnp.zeros_like(out_v)
    span = out_v.shape[1]

    def out_step(owner):
        at = pl.ds(pl.multiple_of(owner * span, span), span)
        out_v[...] += lax.dot_general(
            att_v[owner], wo_v[at, :], (((1,), (1,)), ((), ())), preferred_element_type=F32
        )

    def heads_in(kind, owner):
        def wait(h, carry):
            head_copy(h, kind, owner, n).wait_recv()
            return carry

        lax.fori_loop(0, GROUP, wait, 0)

    heads_in(0, around(3))
    heads_in(1, around(2))
    heads_in(2, around(1))

    def near_step(k, carry):
        out_step(around(k))
        return carry

    lax.fori_loop(0, 4, near_step, 0)
    far_ring = 4 - ring

    def beyond(k):
        return far_ring + lax.rem(n + k, 4)

    heads_in(4, beyond(3))
    heads_in(5, beyond(2))
    heads_in(6, beyond(1))

    def far_step(k, carry):
        out_step(beyond(k))
        return carry

    lax.fori_loop(0, 4, far_step, 0)
    out_ref[...] = out_v[...].astype(BF16)

    def sent(h, carry):
        head_copy(h, 3, n, across).wait_send()
        for kind in range(3):
            head_copy(h, kind, n, around(kind + 1)).wait_send()
            head_copy(h, kind + 4, across, around(kind + 1)).wait_send()
        return carry

    lax.fori_loop(0, GROUP, sent, 0)
    for copy in started:
        copy.wait_send()
    exchange.wait_send()

    @pl.when(has_twin)
    def _():
        twin_copy().wait_send()

    own_page.wait()

    def relay_end(k, carry):
        relay_copy(k, lax.rem(w + k, WIDE), w).wait_send()
        relay_copy(k, w, lax.rem(w - k + WIDE, WIDE)).wait_recv()
        return carry

    lax.fori_loop(1, WIDE, relay_end, 0)


def on_device(
    tokens,
    norm_gain,
    w_query,
    w_keyval,
    w_output,
    prompt_cache,
    stretch_lengths,
    stretch_starts,
    page_route,
):
    tok_rows, depth = tokens.shape
    rows, q_cols = w_query.shape
    layers, kinds, cache_rows, channels = prompt_cache.shape
    pages = page_route.shape[1]
    page_rows = cache_rows // pages
    half = layers // 2
    cols = q_cols + 2 * channels
    wqkv = jnp.concatenate([w_query, w_keyval.reshape(rows, 2 * channels)], 1)
    freq = 1000000.0 ** (-jnp.arange(HEAD // 2, dtype=jnp.float32) * 2.0 / HEAD)
    freq = jnp.concatenate([freq, freq])[None]
    any_spec = pl.BlockSpec(memory_space=pl.ANY)
    vmem_spec = pl.BlockSpec(memory_space=pltpu.VMEM)
    smem_spec = pl.BlockSpec(memory_space=pltpu.SMEM)
    cache5 = prompt_cache.reshape(layers, kinds, pages, page_rows, channels)
    dma = pltpu.SemaphoreType.DMA
    attn_out, relay = pl.pallas_call(
        whole_kernel,
        out_shape=(
            jax.ShapeDtypeStruct((tok_rows, q_cols), BF16),
            jax.ShapeDtypeStruct((1, half, kinds, WIDE, page_rows, 2 * channels), BF16),
        ),
        in_specs=[
            any_spec, vmem_spec, any_spec, any_spec, any_spec, vmem_spec,
            smem_spec, smem_spec, smem_spec,
        ],
        out_specs=(vmem_spec, any_spec),
        scratch_shapes=[
            pltpu.VMEM((tok_rows, depth), BF16),
            pltpu.VMEM((WIDE * rows, cols), BF16),
            pltpu.VMEM((WIDE, kinds, pages, page_rows, channels), BF16),
            pltpu.VMEM((rows, q_cols), BF16),
            pltpu.VMEM((WIDE * rows, q_cols), BF16),
            pltpu.VMEM((half, kinds, pages, page_rows, 2 * channels), BF16),
            pltpu.VMEM((WIDE, half, kinds, page_rows, 2 * channels), BF16),
            pltpu.VMEM((tok_rows, cols), F32),
            pltpu.VMEM((GROUP, tok_rows, HEAD), BF16),
            pltpu.VMEM((BACK + 1, 2, tok_rows, HEAD), BF16),
            pltpu.VMEM((NARROW, tok_rows, q_cols), BF16),
            pltpu.VMEM((tok_rows, HEAD), F32),
            pltpu.VMEM((tok_rows, HEAD), F32),
            pltpu.VMEM((tok_rows, HEAD), F32),
            pltpu.VMEM((tok_rows, HEAD), F32),
            pltpu.VMEM((tok_rows, HEAD), F32),
            pltpu.VMEM((tok_rows, HEAD), jnp.int32),
            pltpu.VMEM((tok_rows, q_cols), F32),
            dma((7,)),
            dma((3, MESSAGES)),
            dma((3, MESSAGES)),
            dma,
            dma,
            dma,
            dma,
            dma((WIDE,)),
            dma((WIDE,)),
            dma((BACK + 1,)),
            dma((BACK + 1,)),
            dma((GROUP, 7)),
            dma((GROUP, 7)),
        ],
        compiler_params=pltpu.CompilerParams(
            collective_id=0, has_side_effects=True, vmem_limit_bytes=60 * 2**20
        ),
    )(
        tokens, norm_gain[None], wqkv, w_output.T, cache5, freq,
        stretch_lengths, stretch_starts, page_route,
    )
    return attn_out, relay


def solution(mesh):
    placed = (
        P("wide", None),
        P(),
        P("wide", "narrow"),
        P("wide", None, "narrow"),
        P("narrow", "wide"),
        P(None, None, "wide", "narrow"),
        P(),
        P(),
        P("wide", None),
    )
    return jax.shard_map(
        on_device,
        mesh=mesh,
        in_specs=placed,
        out_specs=(P("wide", "narrow"), P("narrow", None, None, "wide", None, None)),
        check_vma=False,
    )
```

time: 618 us -> 240 us (0.39)
  waiting for transfers between devices: 291 us -> 0 us
  Pallas kernels: 0 us -> 227 us
  matrix products: 128 us -> 0 us
  other arithmetic: 108 us -> 2.46 us
  local copies, waits for them, and re-layouts: 56.5 us -> 7.59 us
  between operations: 14 us -> 0.65 us
  loops' own time: 11.5 us -> 0 us
    pallas_call x0 -> x1, Pallas kernels: none -> 227 us  [on_device(): pl.pallas_call(whole_kernel, out_shape=(jax.ShapeDtypeStruct((tok_rows, q...]
    all_gather x4 -> x0, waiting for transfers between devices: 164 us -> none  [the longest x1 61.6 us: on_device(): piece = lax.all_gather(keyblock, 'wide', axis=1, tiled=True)]
    dot_general x35 -> x0, matrix products: 128 us -> none  [the longest x16 66.8 us: attend_block(): jnp.einsum('tkgd,skd->kgts', qgroup, keys, preferred_element_type=jnp.flo...]
    reduce_sum x35 -> x0, other arithmetic: 81.1 us -> none  [the longest x16 76.6 us: attend_block(): den = den * factor + jnp.sum(weights, -1)]
    all_to_all x1 -> x0, waiting for transfers between devices: 77.9 us -> none  [relay_pages(): lax.all_to_all(ordered, 'wide', split_axis=2, concat_axis=3, tiled=True)]
    ppermute x1 -> x0, waiting for transfers between devices: 47.5 us -> none  [from_partner(): return lax.ppermute(value, axis, pairs)]
    dynamic_slice x32 -> x0, local copies, waits for them, and re-layouts: 26.4 us -> none  [on_device(): lax.scan(step, carry, (jnp.arange(count, dtype=jnp.int32), parts))]
    or x16 -> x0, other arithmetic: 13.3 us -> none  [attend_block(): is_prompt[None, :]]
  transfers between devices with their start and end apart: 7 -> 0, of which waited for: 5 -> 0; matrix products, arithmetic and copies ran while one was open for 45% -> 0% of each run, Pallas kernels for 0% -> 0%
where the time goes in v1:
time: 240 us; the launch traced here: 237 us
  Pallas kernels  227 us (95%)
  local copies, waits for them, and re-layouts  7.59 us (3%)
  other arithmetic  2.46 us (1%)
    pallas_call x1, Pallas kernels, on_device(): pl.pallas_call(whole_kernel, out_shape=(jax.ShapeDtypeStruct((tok_rows, q...  227 us
    unnamed x3, local copies, waits for them, and re-layouts  7.59 us

profile of v1, /device:TPU:32, one launch (start us, length us, event | category | flops | bytes accessed | tf_op | source)
XLA Modules:
  0.0 237.5 jit_solution(10196524878625619734)
XLA Ops:
  0.6 0.6 maximum_bitcast_fusion.freq_ref
  1.2 0.9 copy.13
  2.2 1.9 pad_maximum_fusion.wqkv_hbm
  4.0 226.8 %shard_map.104 = (bf16[384,640]{1,0:T(8,128)(2,1)}, bf16[1,8,2,16,32,256]{5,4,3,2,1,0:T(8,128)(2,1)}) custom-call(bf16[384,5120]{1,0:T(8,128)(2,1)} %tok_hbm.1, f32[1,5120]{1,0:T(1,128)} %bitcast.13, bf16[320,896]{1,0:T(8,128)(2,1)} %pad_maximum_fusion.wqkv_hbm, bf16[320,640]{1,0:T(8,128)(2,1)} %bitcast.11, bf16[16,2,16,32,128]{4,3,2,1,0:T(8,128)(2,1)} %bitcast.9, ...), custom_call_target="tpu_custom_call" | custom-call | tf_op jit(solution)/shard_map/pallas_call | solution.py:530
  230.8 1.9 copy.16
  232.7 4.8 %copy.17 = bf16[1,8,2,16,32,256]{5,4,3,2,1,0:T(8,128)(2,1)} copy(bf16[1,8,2,16,32,256]{5,4,3,2,1,0:T(8,128)(2,1)} %get-tuple-element.5) | data formatting | bytes 8388608
  (1 shorter events, 0.0 us)

commit v2 on v1

--- a/solution.py
+++ b/solution.py
@@ -19,6 +19,9 @@
 BACK = 4
 LOG2E = 1.4426950408889634
 MESSAGES = 17
+PLANE = 8
+PAIR = 2
+PAIRS = PLANE // PAIR
 
 
 def whole_kernel(
@@ -38,8 +41,11 @@
     kvp_v,
     wot_v,
     wo_v,
-    comb_v,
-    stage_v,
+    cache_v,
+    zsend_v,
+    zrecv_v,
+    xsend_v,
+    ysend_v,
     proj_v,
     q_v,
     nkv_v,
@@ -58,6 +64,10 @@
     t_recv,
     x_send,
     x_recv,
+    z_send,
+    z_recv,
+    f_sem,
+    o_sem,
     r_send,
     r_recv,
     n_send,
@@ -67,9 +77,7 @@
 ):
     tok_rows, depth = x_v.shape
     rows = wqkv_hbm.shape[0]
-    cols = wqkv_hbm.shape[1]
-    page_rows = comb_v.shape[3]
-    half_layers = comb_v.shape[0]
+    half_layers = xsend_v.shape[1]
     w = lax.axis_index("wide")
     n = lax.axis_index("narrow")
     core = lax.rem(w, 2)
@@ -98,11 +106,7 @@
         pltpu.make_async_copy(
             wqkv_hbm, wqkv_v.at[pl.ds(pl.multiple_of(w * rows, 64), rows)], local_sem.at[1]
         ),
-        pltpu.make_async_copy(
-            cache_hbm.at[pl.ds(par * half_layers, half_layers)],
-            comb_v.at[:, :, :, :, pl.ds(half_at, HEAD)],
-            local_sem.at[2],
-        ),
+        pltpu.make_async_copy(cache_hbm, cache_v, local_sem.at[2]),
         pltpu.make_async_copy(cache_hbm.at[0], kvp_v.at[w], local_sem.at[3]),
     ]
     for copy in copies:
@@ -229,14 +233,74 @@
         ):
             arrived(a, kind, sib(chunk))
 
-    exchange = pltpu.make_async_remote_copy(
-        src_ref=cache_hbm.at[pl.ds((1 - par) * half_layers, half_layers)],
-        dst_ref=comb_v.at[:, :, :, :, pl.ds(half_at, HEAD)],
-        send_sem=x_send, recv_sem=x_recv, device_id=(w, partner), device_id_type=MESH,
-    )
     first(0)
     first(1)
-    exchange.start()
+
+    own_half = pl.ds(par * half_layers, half_layers)
+    partner_half = pl.ds((1 - par) * half_layers, half_layers)
+    own_lanes = pl.ds(half_at, HEAD)
+
+    def z_copy(p):
+        at = pl.ds(p * PAIR, PAIR)
+        return pltpu.make_async_remote_copy(
+            src_ref=zsend_v.at[at], dst_ref=zrecv_v.at[at],
+            send_sem=z_send.at[p], recv_sem=z_recv.at[p],
+            device_id=(over_z(w), n), device_id_type=MESH,
+        )
+
+    def near_x_copy():
+        return pltpu.make_async_remote_copy(
+            src_ref=xsend_v, dst_ref=ysend_v.at[0, :, :, :, :, own_lanes],
+            send_sem=x_send.at[PAIRS], recv_sem=x_recv.at[PAIRS],
+            device_id=(w, partner), device_id_type=MESH,
+        )
+
+    def far_x_copy(p):
+        at = pl.ds(p * PAIR, PAIR)
+        return pltpu.make_async_remote_copy(
+            src_ref=zrecv_v.at[at, partner_half], dst_ref=ysend_v.at[1, at, :, :, :, own_lanes],
+            send_sem=x_send.at[p], recv_sem=x_recv.at[p],
+            device_id=(w, partner), device_id_type=MESH,
+        )
+
+    def far_own_copy(p):
+        at = pl.ds(p * PAIR, PAIR)
+        return pltpu.make_async_copy(
+            zrecv_v.at[at, own_half], ysend_v.at[1, at, :, :, :, own_lanes], f_sem.at[p]
+        )
+
+    def page_for(to):
+        page = jnp.int32(0)
+        for t in range(WIDE):
+            page = jnp.where(route_ref[0, t] == to, jnp.int32(t), page)
+        return page
+
+    copies[2].wait()
+
+    def lay_far(d, carry):
+        zsend_v[d] = cache_v[:, :, page_for(over_z(plane) + d)]
+        return carry
+
+    def lay_near(d, carry):
+        page = page_for(plane + d)
+        xsend_v[d] = cache_v[partner_half, :, page]
+        ysend_v[0, d, :, :, :, own_lanes] = cache_v[own_half, :, page]
+        return carry
+
+    def z_step(p, carry):
+        lax.fori_loop(p * PAIR, (p + 1) * PAIR, lay_far, 0)
+        z_copy(p).start()
+        return carry
+
+    lax.fori_loop(0, PAIRS, z_step, 0)
+    lax.fori_loop(0, PLANE, lay_near, 0)
+    near_x_copy().start()
+
+    def to_partner(p, carry):
+        z_copy(p).wait_recv()
+        far_x_copy(p).start()
+        far_own_copy(p).start()
+        return carry
 
     tok_id = w * tok_rows + lax.broadcasted_iota(jnp.int32, (tok_rows, HEAD), 0)
     begin = jnp.zeros((tok_rows, HEAD), jnp.int32)
@@ -303,57 +367,70 @@
     def rotated(heads):
         return (heads * cos_v[...] + pltpu.roll(heads, HEAD // 2, 1) * sin_v[...]).astype(BF16)
 
-    nkv_v[0, 0] = rotated(proj_v[:, GROUP * HEAD : (GROUP + 1) * HEAD])
-    nkv_v[0, 1] = proj_v[:, (GROUP + 1) * HEAD : (GROUP + 2) * HEAD].astype(BF16)
-    back_copies = []
-    for j in range(1, BACK + 1):
-        copy = pltpu.make_async_remote_copy(
-            src_ref=nkv_v.at[0], dst_ref=nkv_v.at[j],
-            send_sem=n_send.at[j], recv_sem=n_recv.at[j],
-            device_id=(lax.rem(w + j, WIDE), n), device_id_type=MESH,
-        )
+    nkv_v[0, core, 0] = rotated(proj_v[:, GROUP * HEAD : (GROUP + 1) * HEAD])
+    nkv_v[0, core, 1] = proj_v[:, (GROUP + 1) * HEAD : (GROUP + 2) * HEAD].astype(BF16)
+
+    def back_copy(kind, slot, slot_to, which, to):
+        return pltpu.make_async_remote_copy(
+            src_ref=nkv_v.at[slot, which], dst_ref=nkv_v.at[slot_to, which],
+            send_sem=n_send.at[kind], recv_sem=n_recv.at[kind],
+            device_id=(to, n), device_id_type=MESH,
+        )
+
+    back_copies = [
+        back_copy(1, 0, 1, core, lax.rem(w + 2, WIDE)),
+        back_copy(2, 0, 2, core, lax.rem(w + 4, WIDE)),
+        back_copy(0, 0, 0, core, sib(w)),
+        back_copy(3, 1, 1, core, sib(w)),
+        back_copy(4, 2, 2, core, sib(w)),
+    ]
+    for copy in back_copies[:3]:
         copy.start()
-        back_copies.append(copy)
     for h in range(GROUP):
         q_v[h] = rotated(proj_v[:, h * HEAD : (h + 1) * HEAD])
 
     fourth(1)
+    lax.fori_loop(0, PAIRS // 2, to_partner, 0)
+    back_copies[0].wait_recv()
+    back_copies[3].start()
     fifth(1)
+    back_copies[1].wait_recv()
+    back_copies[4].start()
     fourth(2)
+    lax.fori_loop(PAIRS // 2, PAIRS, to_partner, 0)
+
+    place = w - plane
+
+    def source_of(s):
+        return w if s == 0 else over_z(w)
+
+    def y_copy(s, k, d, source):
+        return pltpu.make_async_remote_copy(
+            src_ref=ysend_v.at[s, d], dst_ref=relay_ref.at[0, :, :, source],
+            send_sem=r_send.at[s, k], recv_sem=r_recv.at[s, k],
+            device_id=(plane + d, n), device_id_type=MESH,
+        )
+
+    def to_owners(s):
+        def step(k, carry):
+            y_copy(s, k, lax.rem(place + k, PLANE), source_of(s)).start()
+            return carry
+
+        lax.fori_loop(1, PLANE, step, 0)
+
+    def own_page(s):
+        return pltpu.make_async_copy(
+            ysend_v.at[s, place], relay_ref.at[0, :, :, source_of(s)], o_sem.at[s]
+        )
+
+    near_x_copy().wait_recv()
+    to_owners(0)
+    own_page(0).start()
     fifth(2)
-
-    copies[2].wait()
-    exchange.wait_recv()
-
-    def relay_copy(k, to, source):
-        return pltpu.make_async_remote_copy(
-            src_ref=stage_v.at[to], dst_ref=relay_ref.at[0, :, :, source],
-            send_sem=r_send.at[k], recv_sem=r_recv.at[k],
-            device_id=(to, n), device_id_type=MESH,
-        )
-
-    def lay_out(k):
-        to = lax.rem(w + k, WIDE)
-        page = jnp.int32(0)
-        for t in range(WIDE):
-            page = jnp.where(route_ref[0, t] == to, jnp.int32(t), page)
-        stage_v[to] = comb_v[:, :, page]
-        return to
-
-    def relay_step(k, carry):
-        to = lay_out(k)
-        relay_copy(k, to, w).start()
-        return carry
-
-    lax.fori_loop(1, WIDE, relay_step, 0)
-    lay_out(0)
-    own_page = pltpu.make_async_copy(stage_v.at[w], relay_ref.at[0, :, :, w], local_sem.at[6])
-    own_page.start()
-
     finish(1)
     copies[3].wait()
-    for copy in back_copies:
-        copy.wait()
+    for kind, slot, copy in ((0, 0, 2), (3, 1, 3), (4, 2, 4)):
+        back_copy(kind, slot, slot, 1 - core, sib(w)).wait_recv()
 
     factor = HEAD ** (-0.5) * LOG2E
 
@@ -383,18 +460,53 @@
     def around(k):
         return ring + lax.rem(n + k, 4)
 
+    far_ring = 4 - ring
+
+    def beyond(k):
+        return far_ring + lax.rem(n + k, 4)
+
+    lead, trail = around(1), around(3)
+
     def head_copy(h, kind, owner, to):
-        at = att_v.at[owner, :, pl.ds(pl.multiple_of(h * HEAD, HEAD), HEAD)]
+        lanes = pl.ds(pl.multiple_of(h * HEAD, HEAD), HEAD)
+        if kind < 5:
+            at = att_v.at[owner, :, lanes]
+        else:
+            at = att_v.at[owner, pl.ds((kind + 1) % 2 * (tok_rows // 2), tok_rows // 2), lanes]
         return pltpu.make_async_remote_copy(
             src_ref=at, dst_ref=at, send_sem=a_send.at[h, kind], recv_sem=a_recv.at[h, kind],
             device_id=(w, to), device_id_type=MESH,
         )
 
-    def forward(h):
-        head_copy(h, 3, across, n).wait_recv()
-        head_copy(h, 4, across, around(1)).start()
-        head_copy(h, 5, across, around(2)).start()
-        head_copy(h, 6, across, around(3)).start()
+    sends = (
+        (0, n, lead, trail), (1, n, trail, lead), (2, n, across, across),
+        (3, across, lead, beyond(3)), (4, across, trail, beyond(1)),
+        (5, trail, lead, around(2)), (6, lead, trail, around(2)),
+        (7, beyond(3), lead, beyond(2)), (8, beyond(1), trail, beyond(2)),
+    )
+
+    def give(h, *kinds):
+        for kind in kinds:
+            _, owner, to, _ = sends[kind]
+            head_copy(h, kind, owner, to).start()
+
+    def take(h, *kinds):
+        for kind in kinds:
+            head_copy(h, kind, sends[kind][3], n).wait_recv()
+
+    def pass_on(h):
+        take(h, 2)
+        give(h, 3, 4)
+        take(h, 0)
+        give(h, 5)
+        take(h, 1)
+        give(h, 6)
+
+    def pass_further(h):
+        take(h, 3)
+        give(h, 7)
+        take(h, 4)
+        give(h, 8)
 
     def head_step(h, carry):
         top_v[...] = jnp.full_like(top_v, -1e30)
@@ -412,93 +524,101 @@
             key_id = (w - j) * tok_rows + lax.broadcasted_iota(jnp.int32, (tok_rows, tok_rows), 1)
             own_id = w * tok_rows + lax.broadcasted_iota(jnp.int32, (tok_rows, tok_rows), 0)
             visible = (key_id >= begin_v[:, :1]) & (key_id <= own_id)
-            attend(h, nkv_v[j, 0], nkv_v[j, 1], visible)
+            source = lax.rem(w - j + WIDE, WIDE)
+            away = lax.rem(w // 2 - source // 2 + PLANE, PLANE)
+            which = lax.rem(source, 2)
+            attend(h, nkv_v[away, which, 0], nkv_v[away, which, 1], visible)
             return inner
 
         lax.fori_loop(0, BACK + 1, new_step, 0)
         den = jnp.sum(den_v[...], 1, keepdims=True)
         att_v[n, :, pl.ds(pl.multiple_of(h * HEAD, HEAD), HEAD)] = (acc_v[...] / den).astype(BF16)
-        head_copy(h, 3, n, across).start()
-        head_copy(h, 0, n, around(1)).start()
-        head_copy(h, 1, n, around(2)).start()
-        head_copy(h, 2, n, around(3)).start()
+        give(h, 2, 0, 1)
+
+        @pl.when(h == 0)
+        def _():
+            def far_ready(p, inner):
+                far_x_copy(p).wait_recv()
+                far_own_copy(p).wait()
+                return inner
+
+            lax.fori_loop(0, PAIRS, far_ready, 0)
+            to_owners(1)
+            own_page(1).start()
 
         @pl.when(h > 0)
         def _():
-            forward(h - 1)
+            pass_on(h - 1)
+
+        @pl.when(h > 1)
+        def _():
+            pass_further(h - 2)
 
         return carry
 
     lax.fori_loop(0, GROUP, head_step, 0)
-    forward(GROUP - 1)
+    last = GROUP - 1
+    pass_further(last - 1)
+    pass_on(last)
 
     finish(2)
     own_wo2.wait()
     out_v[...] = jnp.zeros_like(out_v)
     span = out_v.shape[1]
 
-    def out_step(owner):
-        at = pl.ds(pl.multiple_of(owner * span, span), span)
+    early = last * HEAD
+
+    def earlier(h, carry):
+        take(h, 5, 6, 7, 8)
+        return carry
+
+    lax.fori_loop(0, last, earlier, 0)
+
+    def out_step(owner, carry, at=0, size=early):
+        rows_at = pl.ds(pl.multiple_of(owner * span, span), span)
         out_v[...] += lax.dot_general(
-            att_v[owner], wo_v[at, :], (((1,), (1,)), ((), ())), preferred_element_type=F32
-        )
-
-    def heads_in(kind, owner):
-        def wait(h, carry):
-            head_copy(h, kind, owner, n).wait_recv()
-            return carry
-
-        lax.fori_loop(0, GROUP, wait, 0)
-
-    heads_in(0, around(3))
-    heads_in(1, around(2))
-    heads_in(2, around(1))
-
-    def near_step(k, carry):
-        out_step(around(k))
-        return carry
-
-    lax.fori_loop(0, 4, near_step, 0)
-    far_ring = 4 - ring
-
-    def beyond(k):
-        return far_ring + lax.rem(n + k, 4)
-
-    heads_in(4, beyond(3))
-    heads_in(5, beyond(2))
-    heads_in(6, beyond(1))
-
-    def far_step(k, carry):
-        out_step(beyond(k))
-        return carry
-
-    lax.fori_loop(0, 4, far_step, 0)
+            att_v[owner, :, at : at + size], wo_v[rows_at, at : at + size],
+            (((1,), (1,)), ((), ())), preferred_element_type=F32,
+        )
+        return carry
+
+    lax.fori_loop(0, NARROW // 2, out_step, 0)
+    pass_further(last)
+    lax.fori_loop(NARROW // 2, NARROW, out_step, 0)
+    take(last, 5, 6, 7, 8)
+    lax.fori_loop(0, NARROW, lambda owner, carry: out_step(owner, carry, early, HEAD), 0)
     out_ref[...] = out_v[...].astype(BF16)
 
     def sent(h, carry):
-        head_copy(h, 3, n, across).wait_send()
-        for kind in range(3):
-            head_copy(h, kind, n, around(kind + 1)).wait_send()
-            head_copy(h, kind + 4, across, around(kind + 1)).wait_send()
+        for kind, owner, to, _ in sends:
+            head_copy(h, kind, owner, to).wait_send()
         return carry
 
     lax.fori_loop(0, GROUP, sent, 0)
-    for copy in started:
+    for copy in started + back_copies:
         copy.wait_send()
-    exchange.wait_send()
 
     @pl.when(has_twin)
     def _():
         twin_copy().wait_send()
 
-    own_page.wait()
-
-    def relay_end(k, carry):
-        relay_copy(k, lax.rem(w + k, WIDE), w).wait_send()
-        relay_copy(k, w, lax.rem(w - k + WIDE, WIDE)).wait_recv()
-        return carry
-
-    lax.fori_loop(1, WIDE, relay_end, 0)
+    def far_sent(p, carry):
+        z_copy(p).wait_send()
+        far_x_copy(p).wait_send()
+        return carry
+
+    lax.fori_loop(0, PAIRS, far_sent, 0)
+    near_x_copy().wait_send()
+    for s in range(2):
+        own_page(s).wait()
+
+        def relay_end(k, carry):
+            y_copy(s, k, lax.rem(place + k, PLANE), source_of(s)).wait_send()
+            giver = plane + lax.rem(place - k + PLANE, PLANE)
+            y_copy(s, k, place, giver if s == 0 else over_z(giver)).wait_recv()
+            return carry
+
+        lax.fori_loop(1, PLANE, relay_end, 0)
 
 
 def on_device(
@@ -544,11 +664,14 @@
             pltpu.VMEM((WIDE, kinds, pages, page_rows, channels), BF16),
             pltpu.VMEM((rows, q_cols), BF16),
             pltpu.VMEM((WIDE * rows, q_cols), BF16),
-            pltpu.VMEM((half, kinds, pages, page_rows, 2 * channels), BF16),
-            pltpu.VMEM((WIDE, half, kinds, page_rows, 2 * channels), BF16),
+            pltpu.VMEM((layers, kinds, pages, page_rows, channels), BF16),
+            pltpu.VMEM((PLANE, layers, kinds, page_rows, channels), BF16),
+            pltpu.VMEM((PLANE, layers, kinds, page_rows, channels), BF16),
+            pltpu.VMEM((PLANE, half, kinds, page_rows, channels), BF16),
+            pltpu.VMEM((2, PLANE, half, kinds, page_rows, 2 * channels), BF16),
             pltpu.VMEM((tok_rows, cols), F32),
             pltpu.VMEM((GROUP, tok_rows, HEAD), BF16),
-            pltpu.VMEM((BACK + 1, 2, tok_rows, HEAD), BF16),
+            pltpu.VMEM((3, 2, 2, tok_rows, HEAD), BF16),
             pltpu.VMEM((NARROW, tok_rows, q_cols), BF16),
             pltpu.VMEM((tok_rows, HEAD), F32),
             pltpu.VMEM((tok_rows, HEAD), F32),
@@ -557,19 +680,23 @@
             pltpu.VMEM((tok_rows, HEAD), F32),
             pltpu.VMEM((tok_rows, HEAD), jnp.int32),
             pltpu.VMEM((tok_rows, q_cols), F32),
-            dma((7,)),
+            dma((6,)),
             dma((3, MESSAGES)),
             dma((3, MESSAGES)),
             dma,
             dma,
-            dma,
-            dma,
-            dma((WIDE,)),
-            dma((WIDE,)),
-            dma((BACK + 1,)),
-            dma((BACK + 1,)),
-            dma((GROUP, 7)),
-            dma((GROUP, 7)),
+            dma((PAIRS + 1,)),
+            dma((PAIRS + 1,)),
+            dma((PAIRS,)),
+            dma((PAIRS,)),
+            dma((PAIRS,)),
+            dma((2,)),
+            dma((2, PLANE)),
+            dma((2, PLANE)),
+            dma((5,)),
+            dma((5,)),
+            dma((GROUP, 9)),
+            dma((GROUP, 9)),
         ],
         compiler_params=pltpu.CompilerParams(
             collective_id=0, has_side_effects=True, vmem_limit_bytes=60 * 2**20

time: 240 us -> 249 us (1.038)
  the two profiles are of different devices: /device:TPU:32 before, /device:TPU:24 now
where the time goes in v2:
time: 249 us; the launch traced here: 248 us
  Pallas kernels  238 us (96%)
  local copies, waits for them, and re-layouts  7.59 us (3%)
    pallas_call x1, Pallas kernels, on_device(): pl.pallas_call(whole_kernel, out_shape=(jax.ShapeDtypeStruct((tok_rows, q...  238 us
    unnamed x3, local copies, waits for them, and re-layouts  7.59 us

profile of v2, /device:TPU:24, one launch (start us, length us, event | category | flops | bytes accessed | tf_op | source)
XLA Modules:
  0.0 248.2 jit_solution(16264003918778059302)
XLA Ops:
  0.6 0.6 maximum_bitcast_fusion.freq_ref
  1.2 0.9 copy.13
  2.2 1.9 pad_maximum_fusion.wqkv_hbm
  4.0 237.5 %shard_map.104 = (bf16[384,640]{1,0:T(8,128)(2,1)}, bf16[1,8,2,16,32,256]{5,4,3,2,1,0:T(8,128)(2,1)}) custom-call(bf16[384,5120]{1,0:T(8,128)(2,1)} %tok_hbm.1, f32[1,5120]{1,0:T(1,128)} %bitcast.13, bf16[320,896]{1,0:T(8,128)(2,1)} %pad_maximum_fusion.wqkv_hbm, bf16[320,640]{1,0:T(8,128)(2,1)} %bitcast.11, bf16[16,2,16,32,128]{4,3,2,1,0:T(8,128)(2,1)} %bitcast.9, ...), custom_call_target="tpu_custom_call" | custom-call | tf_op jit(solution)/shard_map/pallas_call | solution.py:650
  241.6 1.9 copy.16
  243.4 4.8 %copy.17 = bf16[1,8,2,16,32,256]{5,4,3,2,1,0:T(8,128)(2,1)} copy(bf16[1,8,2,16,32,256]{5,4,3,2,1,0:T(8,128)(2,1)} %get-tuple-element.5) | data formatting | bytes 8388608
  (1 shorter events, 0.0 us)

commit v3 on v2

--- a/solution.py
+++ b/solution.py
@@ -15,7 +15,7 @@
 NARROW = 8
 BF16 = jnp.bfloat16
 F32 = jnp.float32
-KEYS = 1024
+KEYS = 2048
 BACK = 4
 LOG2E = 1.4426950408889634
 MESSAGES = 17
@@ -39,6 +39,7 @@
     x_v,
     wqkv_v,
     kvp_v,
+    wos_v,
     wot_v,
     wo_v,
     cache_v,
@@ -95,10 +96,19 @@
         return lax.rem(chunk + 8, 16)
 
     yr, yl, y2 = at_y(1), at_y(3), at_y(2)
+    zw, zr, zl, z2 = over_z(w), over_z(yr), over_z(yl), over_z(y2)
+    sw = sib(w)
     par = lax.rem(n, 2)
     partner = n + 1 - 2 * par
-    twin_w, twin_n = 2 * n + core, w // 2
-    has_twin = twin_n != n
+    x_at, z_at = lax.rem(n, 4), n // 4
+
+    def mix(one, other):
+        return one + other - 2 * one * other
+
+    shift_w = mix(zh, z_at) * 8 + lax.rem(y + x_at, 4) * 2 + core
+    shifts = n > 0
+    turn_n = mix(zh, z_at) * 4 + lax.rem(y - x_at + 4, 4)
+    turns = turn_n != n
 
     half_at = pl.multiple_of(par * HEAD, HEAD)
     copies = [
@@ -125,32 +135,36 @@
     lax.fori_loop(1, WIDE, greet_wide, 0)
     lax.fori_loop(1, NARROW, greet_narrow, 0)
 
-    peers = WIDE - 1 + NARROW - 1
-
-    @pl.when(has_twin)
-    def _():
-        pl.semaphore_signal(barrier, inc=1, device_id=(twin_w, twin_n), device_id_type=MESH)
-        pl.semaphore_wait(barrier, peers + 1)
-
-    @pl.when(jnp.logical_not(has_twin))
-    def _():
-        pl.semaphore_wait(barrier, peers)
-
-    def twin_copy():
-        return pltpu.make_async_remote_copy(
-            src_ref=wo_hbm, dst_ref=wot_v, send_sem=t_send, recv_sem=t_recv,
-            device_id=(twin_w, twin_n), device_id_type=MESH,
-        )
-
-    own_wo = pltpu.make_async_copy(wo_hbm, wot_v, local_sem.at[4])
-
-    @pl.when(has_twin)
-    def _():
-        twin_copy().start()
-
-    @pl.when(jnp.logical_not(has_twin))
-    def _():
-        own_wo.start()
+    pl.semaphore_wait(barrier, WIDE - 1 + NARROW - 1)
+
+    def shift_copy():
+        return pltpu.make_async_remote_copy(
+            src_ref=wo_hbm, dst_ref=wos_v, send_sem=t_send.at[0], recv_sem=t_recv.at[0],
+            device_id=(shift_w, n), device_id_type=MESH,
+        )
+
+    def turn_copy():
+        return pltpu.make_async_remote_copy(
+            src_ref=wos_v, dst_ref=wot_v, send_sem=t_send.at[1], recv_sem=t_recv.at[1],
+            device_id=(w, turn_n), device_id_type=MESH,
+        )
+
+    def shift_here():
+        return pltpu.make_async_copy(wo_hbm, wos_v, local_sem.at[4])
+
+    def turn_here():
+        return pltpu.make_async_copy(wos_v, wot_v, local_sem.at[6])
+
+    def either(moves, far, here):
+        @pl.when(moves)
+        def _():
+            far()
+
+        @pl.when(jnp.logical_not(moves))
+        def _():
+            here()
+
+    either(shifts, lambda: shift_copy().start(), lambda: shift_here().start())
 
     def row_view(ref):
         def view(chunk, part=None):
@@ -180,51 +194,47 @@
         )
 
     def send(a, kind, chunk, part, to, own=False):
-        copy = message(a, kind, chunk, part, to, own)
-        copy.start()
-        started.append(copy)
+        message(a, kind, chunk, part, to, own).start()
+        started.append((a, kind, chunk, part, to, own))
 
     def arrived(a, kind, chunk, part=None):
         message(a, kind, chunk, part, w).wait_recv()
 
     def first(a):
-        send(a, 1, w, None, over_z(w), True)
+        send(a, 1, w, None, zw, True)
         send(a, 2, w, None, yr, True)
         send(a, 3, w, None, yl, True)
-        send(a, 0, w, None, sib(w), True)
+        send(a, 0, w, None, sw, True)
 
     def second(a):
-        chunk = over_z(w)
-        arrived(a, 1, chunk)
-        send(a, 5, chunk, None, yr)
-        send(a, 6, chunk, None, yl)
-        send(a, 4, chunk, None, sib(w))
+        arrived(a, 1, zw)
+        send(a, 5, zw, None, yr)
+        send(a, 6, zw, None, yl)
+        send(a, 4, zw, None, sw)
 
     def third(a):
         arrived(a, 2, yl)
         send(a, 8, yl, 0, yr)
-        send(a, 7, yl, None, sib(w))
+        send(a, 7, yl, None, sw)
         arrived(a, 3, yr)
         send(a, 10, yr, 1, yl)
-        send(a, 9, yr, None, sib(w))
+        send(a, 9, yr, None, sw)
 
     def fourth(a):
-        left, right = over_z(yl), over_z(yr)
-        arrived(a, 5, left)
-        send(a, 12, left, 0, yr)
-        send(a, 11, left, None, sib(w))
-        arrived(a, 6, right)
-        send(a, 14, right, 1, yl)
-        send(a, 13, right, None, sib(w))
+        arrived(a, 5, zl)
+        send(a, 12, zl, 0, yr)
+        send(a, 11, zl, None, sw)
+        arrived(a, 6, zr)
+        send(a, 14, zr, 1, yl)
+        send(a, 13, zr, None, sw)
 
     def fifth(a):
         arrived(a, 8, y2, 0)
         arrived(a, 10, y2, 1)
-        send(a, 15, y2, None, sib(w))
-        far = over_z(y2)
-        arrived(a, 12, far, 0)
-        arrived(a, 14, far, 1)
-        send(a, 16, far, None, sib(w))
+        send(a, 15, y2, None, sw)
+        arrived(a, 12, z2, 0)
+        arrived(a, 14, z2, 1)
+        send(a, 16, z2, None, sw)
 
     def finish(a):
         for kind, chunk in (
@@ -287,14 +297,8 @@
         ysend_v[0, d, :, :, :, own_lanes] = cache_v[own_half, :, page]
         return carry
 
-    def z_step(p, carry):
-        lax.fori_loop(p * PAIR, (p + 1) * PAIR, lay_far, 0)
-        z_copy(p).start()
-        return carry
-
-    lax.fori_loop(0, PAIRS, z_step, 0)
+    lax.fori_loop(0, PLANE, lay_far, 0)
     lax.fori_loop(0, PLANE, lay_near, 0)
-    near_x_copy().start()
 
     def to_partner(p, carry):
         z_copy(p).wait_recv()
@@ -331,28 +335,27 @@
 
     lax.fori_loop(0, tok_rows // block, norm_block, 0)
 
+    either(shifts, lambda: shift_copy().wait_recv(), lambda: shift_here().wait())
+    either(turns, lambda: turn_copy().start(), lambda: turn_here().start())
     second(0)
     third(0)
-
-    @pl.when(has_twin)
-    def _():
-        twin_copy().wait_recv()
-
-    @pl.when(jnp.logical_not(has_twin))
-    def _():
-        own_wo.wait()
-
+    z_copy(0).start()
+    second(1)
+    fourth(0)
+    third(1)
+    z_copy(1).start()
+    either(turns, lambda: turn_copy().wait_recv(), lambda: turn_here().wait())
     first(2)
     own_wo2 = pltpu.make_async_copy(wot_v, views[2](w), local_sem.at[5])
     own_wo2.start()
-    second(1)
-    fourth(0)
-    third(1)
-    second(2)
+    near_x_copy().start()
     fifth(0)
-    third(2)
     finish(0)
     copies[1].wait()
+    fourth(1)
+    second(2)
+    z_copy(2).start()
+    z_copy(3).start()
 
     proj_v[...] = jnp.zeros_like(proj_v)
     step = 1280
@@ -364,8 +367,9 @@
 
     lax.fori_loop(0, depth // step, project, 0)
 
-    def rotated(heads):
-        return (heads * cos_v[...] + pltpu.roll(heads, HEAD // 2, 1) * sin_v[...]).astype(BF16)
+    def rotated(heads, times=1.0):
+        turned = heads * cos_v[...] + pltpu.roll(heads, HEAD // 2, 1) * sin_v[...]
+        return (turned * times).astype(BF16)
 
     nkv_v[0, core, 0] = rotated(proj_v[:, GROUP * HEAD : (GROUP + 1) * HEAD])
     nkv_v[0, core, 1] = proj_v[:, (GROUP + 1) * HEAD : (GROUP + 2) * HEAD].astype(BF16)
@@ -386,18 +390,17 @@
     ]
     for copy in back_copies[:3]:
         copy.start()
+    factor = HEAD ** (-0.5) * LOG2E
     for h in range(GROUP):
-        q_v[h] = rotated(proj_v[:, h * HEAD : (h + 1) * HEAD])
-
-    fourth(1)
-    lax.fori_loop(0, PAIRS // 2, to_partner, 0)
+        q_v[h] = rotated(proj_v[:, h * HEAD : (h + 1) * HEAD], factor)
+
+    third(2)
     back_copies[0].wait_recv()
     back_copies[3].start()
     fifth(1)
     back_copies[1].wait_recv()
     back_copies[4].start()
-    fourth(2)
-    lax.fori_loop(PAIRS // 2, PAIRS, to_partner, 0)
+    lax.fori_loop(0, PAIRS // 2, to_partner, 0)
 
     place = w - plane
 
@@ -426,31 +429,23 @@
     near_x_copy().wait_recv()
     to_owners(0)
     own_page(0).start()
-    fifth(2)
     finish(1)
     copies[3].wait()
     for kind, slot, copy in ((0, 0, 2), (3, 1, 3), (4, 2, 4)):
         back_copy(kind, slot, slot, 1 - core, sib(w)).wait_recv()
 
-    factor = HEAD ** (-0.5) * LOG2E
-
-    def attend(h, keys, vals, visible):
-        score = lax.dot_general(
-            q_v[h], keys, (((1,), (1,)), ((), ())), preferred_element_type=F32
-        ) * factor
-        if visible is not None:
-            score = jnp.where(visible, score, -1e30)
+    def scores(h, keys):
+        return lax.dot_general(q_v[h], keys, (((1,), (1,)), ((), ())), preferred_element_type=F32)
+
+    def attend(score, vals):
         top = top_v[...]
         new_top = jnp.maximum(top, jnp.max(score, 1, keepdims=True))
         fall = jnp.exp2(top - new_top)
-        weight = jnp.exp2(score - new_top[:, :1])
-        part = weight[:, :HEAD]
-        for i in range(1, weight.shape[1] // HEAD):
-            part = part + weight[:, i * HEAD : (i + 1) * HEAD]
-        den_v[...] = den_v[...] * fall + part
-        acc_v[...] = acc_v[...] * fall + jnp.dot(
-            weight.astype(BF16), vals, preferred_element_type=F32
-        )
+        weight = jnp.exp2(score - new_top[:, :1]).astype(BF16)
+        both = jnp.concatenate([vals, jnp.ones(vals.shape, BF16)], 1)
+        summed = jnp.dot(weight, both, preferred_element_type=F32)
+        acc_v[...] = acc_v[...] * fall + summed[:, :HEAD]
+        den_v[...] = den_v[...] * fall + summed[:, HEAD:]
         top_v[...] = new_top
 
     per_step = KEYS // block_keys
@@ -515,28 +510,39 @@
 
         def prompt_step(i, inner):
             at = pl.ds(i * per_step, per_step)
-            attend(h, kvp_v[at, 0].reshape(KEYS, HEAD), kvp_v[at, 1].reshape(KEYS, HEAD), None)
+            attend(scores(h, kvp_v[at, 0].reshape(KEYS, HEAD)), kvp_v[at, 1].reshape(KEYS, HEAD))
             return inner
 
         lax.fori_loop(0, WIDE // per_step, prompt_step, 0)
 
-        def new_step(j, inner):
+        slots = []
+        for j in range(BACK + 1):
+            source = lax.rem(w - j + WIDE, WIDE)
+            slots.append((lax.rem(w // 2 - source // 2 + PLANE, PLANE), lax.rem(source, 2)))
+        new_keys = jnp.concatenate([nkv_v[away, which, 0] for away, which in slots], 0)
+        new_vals = jnp.concatenate([nkv_v[away, which, 1] for away, which in slots], 0)
+        score = scores(h, new_keys)
+        own_id = w * tok_rows + lax.broadcasted_iota(jnp.int32, (tok_rows, tok_rows), 0)
+        masked = []
+        for j in range(BACK + 1):
             key_id = (w - j) * tok_rows + lax.broadcasted_iota(jnp.int32, (tok_rows, tok_rows), 1)
-            own_id = w * tok_rows + lax.broadcasted_iota(jnp.int32, (tok_rows, tok_rows), 0)
-            visible = (key_id >= begin_v[:, :1]) & (key_id <= own_id)
-            source = lax.rem(w - j + WIDE, WIDE)
-            away = lax.rem(w // 2 - source // 2 + PLANE, PLANE)
-            which = lax.rem(source, 2)
-            attend(h, nkv_v[away, which, 0], nkv_v[away, which, 1], visible)
-            return inner
-
-        lax.fori_loop(0, BACK + 1, new_step, 0)
-        den = jnp.sum(den_v[...], 1, keepdims=True)
-        att_v[n, :, pl.ds(pl.multiple_of(h * HEAD, HEAD), HEAD)] = (acc_v[...] / den).astype(BF16)
+            visible = key_id >= begin_v[:, :1]
+            if j == 0:
+                visible = visible & (key_id <= own_id)
+            masked.append(jnp.where(visible, score[:, j * tok_rows : (j + 1) * tok_rows], -1e30))
+        attend(jnp.concatenate(masked, 1), new_vals)
+        att_v[n, :, pl.ds(pl.multiple_of(h * HEAD, HEAD), HEAD)] = (acc_v[...] / den_v[...]).astype(BF16)
         give(h, 2, 0, 1)
 
         @pl.when(h == 0)
         def _():
+            fourth(2)
+            lax.fori_loop(PAIRS // 2, PAIRS, to_partner, 0)
+
+        @pl.when(h == 1)
+        def _():
+            fifth(2)
+
             def far_ready(p, inner):
                 far_x_copy(p).wait_recv()
                 far_own_copy(p).wait()
@@ -575,7 +581,8 @@
     lax.fori_loop(0, last, earlier, 0)
 
     def out_step(owner, carry, at=0, size=early):
-        rows_at = pl.ds(pl.multiple_of(owner * span, span), span)
+        held = mix(owner // 4, z_at) * 4 + lax.rem(owner + x_at, 4)
+        rows_at = pl.ds(pl.multiple_of(held * span, span), span)
         out_v[...] += lax.dot_general(
             att_v[owner, :, at : at + size], wo_v[rows_at, at : at + size],
             (((1,), (1,)), ((), ())), preferred_element_type=F32,
@@ -595,12 +602,13 @@
         return carry
 
     lax.fori_loop(0, GROUP, sent, 0)
-    for copy in started + back_copies:
+    for sending in started:
+        message(*sending).wait_send()
+    for copy in back_copies:
         copy.wait_send()
 
-    @pl.when(has_twin)
-    def _():
-        twin_copy().wait_send()
+    either(shifts, lambda: shift_copy().wait_send(), lambda: None)
+    either(turns, lambda: turn_copy().wait_send(), lambda: None)
 
     def far_sent(p, carry):
         z_copy(p).wait_send()
@@ -663,6 +671,7 @@
             pltpu.VMEM((WIDE * rows, cols), BF16),
             pltpu.VMEM((WIDE, kinds, pages, page_rows, channels), BF16),
             pltpu.VMEM((rows, q_cols), BF16),
+            pltpu.VMEM((rows, q_cols), BF16),
             pltpu.VMEM((WIDE * rows, q_cols), BF16),
             pltpu.VMEM((layers, kinds, pages, page_rows, channels), BF16),
             pltpu.VMEM((PLANE, layers, kinds, page_rows, channels), BF16),
@@ -680,11 +689,11 @@
             pltpu.VMEM((tok_rows, HEAD), F32),
             pltpu.VMEM((tok_rows, HEAD), jnp.int32),
             pltpu.VMEM((tok_rows, q_cols), F32),
-            dma((6,)),
+            dma((7,)),
             dma((3, MESSAGES)),
             dma((3, MESSAGES)),
-            dma,
-            dma,
+            dma((2,)),
+            dma((2,)),
             dma((PAIRS + 1,)),
             dma((PAIRS + 1,)),
             dma((PAIRS,)),

time: 249 us -> 201 us (0.81)
  the two profiles are of different devices: /device:TPU:24 before, /device:TPU:32 now
where the time goes in v3:
time: 201 us
  Pallas kernels  190 us (95%)
  local copies, waits for them, and re-layouts  7.59 us (4%)
  other arithmetic  2.46 us (1%)
    pallas_call x1, Pallas kernels, on_device(): pl.pallas_call(whole_kernel, out_shape=(jax.ShapeDtypeStruct((tok_rows, q...  190 us
    unnamed x3, local copies, waits for them, and re-layouts  7.59 us

profile of v3, /device:TPU:32, one launch (start us, length us, event | category | flops | bytes accessed | tf_op | source)
XLA Modules:
  0.0 200.8 jit_solution(16549350579037279574)
XLA Ops:
  0.6 0.6 maximum_bitcast_fusion.freq_ref
  1.2 0.9 copy.13
  2.2 1.9 pad_maximum_fusion.wqkv_hbm
  4.0 190.1 %shard_map.104 = (bf16[384,640]{1,0:T(8,128)(2,1)}, bf16[1,8,2,16,32,256]{5,4,3,2,1,0:T(8,128)(2,1)}) custom-call(bf16[384,5120]{1,0:T(8,128)(2,1)} %tok_hbm.1, f32[1,5120]{1,0:T(1,128)} %bitcast.13, bf16[320,896]{1,0:T(8,128)(2,1)} %pad_maximum_fusion.wqkv_hbm, bf16[320,640]{1,0:T(8,128)(2,1)} %bitcast.11, bf16[16,2,16,32,128]{4,3,2,1,0:T(8,128)(2,1)} %bitcast.9, ...), custom_call_target="tpu_custom_call" | custom-call | tf_op jit(solution)/shard_map/pallas_call | solution.py:658
  194.1 1.9 copy.16
  196.0 4.8 %copy.17 = bf16[1,8,2,16,32,256]{5,4,3,2,1,0:T(8,128)(2,1)} copy(bf16[1,8,2,16,32,256]{5,4,3,2,1,0:T(8,128)(2,1)} %get-tuple-element.5) | data formatting | bytes 8388608
  (1 shorter events, 0.0 us)

commit v4 on v3

--- a/solution.py
+++ b/solution.py
@@ -508,12 +508,13 @@
         den_v[...] = jnp.zeros_like(den_v)
         acc_v[...] = jnp.zeros_like(acc_v)
 
-        def prompt_step(i, inner):
-            at = pl.ds(i * per_step, per_step)
-            attend(scores(h, kvp_v[at, 0].reshape(KEYS, HEAD)), kvp_v[at, 1].reshape(KEYS, HEAD))
-            return inner
-
-        lax.fori_loop(0, WIDE // per_step, prompt_step, 0)
+        steps = WIDE // per_step
+
+        def keys_at(i):
+            return kvp_v[i * per_step : (i + 1) * per_step, 0].reshape(KEYS, HEAD)
+
+        def vals_at(i):
+            return kvp_v[i * per_step : (i + 1) * per_step, 1].reshape(KEYS, HEAD)
 
         slots = []
         for j in range(BACK + 1):
@@ -521,7 +522,12 @@
             slots.append((lax.rem(w // 2 - source // 2 + PLANE, PLANE), lax.rem(source, 2)))
         new_keys = jnp.concatenate([nkv_v[away, which, 0] for away, which in slots], 0)
         new_vals = jnp.concatenate([nkv_v[away, which, 1] for away, which in slots], 0)
-        score = scores(h, new_keys)
+        ahead = scores(h, keys_at(0))
+        for i in range(steps):
+            score = ahead
+            ahead = scores(h, keys_at(i + 1) if i + 1 < steps else new_keys)
+            attend(score, vals_at(i))
+        score = ahead
         own_id = w * tok_rows + lax.broadcasted_iota(jnp.int32, (tok_rows, tok_rows), 0)
         masked = []
         for j in range(BACK + 1):

time: 201 us -> 186 us (0.925)
  Pallas kernels: 190 us -> 175 us
    pallas_call x1, Pallas kernels: 190 us -> 175 us  [on_device(): pl.pallas_call(whole_kernel, out_shape=(jax.ShapeDtypeStruct((tok_rows, q...]
where the time goes in v4:
time: 186 us
  Pallas kernels  175 us (94%)
  local copies, waits for them, and re-layouts  7.59 us (4%)
  other arithmetic  2.46 us (1%)
    pallas_call x1, Pallas kernels, on_device(): pl.pallas_call(whole_kernel, out_shape=(jax.ShapeDtypeStruct((tok_rows, q...  175 us
    unnamed x3, local copies, waits for them, and re-layouts  7.59 us

profile of v4, /device:TPU:32, one launch (start us, length us, event | category | flops | bytes accessed | tf_op | source)
XLA Modules:
  0.0 185.6 jit_solution(4099367870243330846)
XLA Ops:
  0.6 0.6 maximum_bitcast_fusion.freq_ref
  1.2 0.9 copy.13
  2.2 1.9 %pad_maximum_fusion.wqkv_hbm = bf16[320,896]{1,0:T(8,128)(2,1)} fusion(bf16[320,256]{1,0:T(8,128)(2,1)S(1)} %bitcast.10, bf16[320,640]{1,0:T(8,128)(2,1)} %param.11), kind=kLoop, calls=%fused_computation | loop fusion | flops 1146880 | bytes 1146880 | tf_op jit(solution)/shard_map/concatenate | solution.py:656
  4.0 174.9 %shard_map.104 = (bf16[384,640]{1,0:T(8,128)(2,1)}, bf16[1,8,2,16,32,256]{5,4,3,2,1,0:T(8,128)(2,1)}) custom-call(bf16[384,5120]{1,0:T(8,128)(2,1)} %tok_hbm.1, f32[1,5120]{1,0:T(1,128)} %bitcast.13, bf16[320,896]{1,0:T(8,128)(2,1)} %pad_maximum_fusion.wqkv_hbm, bf16[320,640]{1,0:T(8,128)(2,1)} %bitcast.11, bf16[16,2,16,32,128]{4,3,2,1,0:T(8,128)(2,1)} %bitcast.9, ...), custom_call_target="tpu_custom_call" | custom-call | tf_op jit(solution)/shard_map/pallas_call | solution.py:664
  179.0 1.9 copy.16
  180.8 4.8 %copy.17 = bf16[1,8,2,16,32,256]{5,4,3,2,1,0:T(8,128)(2,1)} copy(bf16[1,8,2,16,32,256]{5,4,3,2,1,0:T(8,128)(2,1)} %get-tuple-element.5) | data formatting | bytes 8388608
  (1 shorter events, 0.0 us)

commit v5 on v4

--- a/solution.py
+++ b/solution.py
@@ -2,6 +2,7 @@
 
 import jax
 import jax.numpy as jnp
+import numpy as np
 from jax import lax
 from jax.experimental import pallas as pl
 from jax.experimental.pallas import tpu as pltpu
@@ -27,7 +28,8 @@
 def whole_kernel(
     tok_hbm,
     gain_ref,
-    wqkv_hbm,
+    wq_hbm,
+    wkv_hbm,
     wo_hbm,
     cache_hbm,
     freq_ref,
@@ -77,7 +79,8 @@
     a_recv,
 ):
     tok_rows, depth = x_v.shape
-    rows = wqkv_hbm.shape[0]
+    rows, q_cols = wq_hbm.shape
+    own_rows = pl.ds(pl.multiple_of(lax.axis_index("wide") * rows, 64), rows)
     half_layers = xsend_v.shape[1]
     w = lax.axis_index("wide")
     n = lax.axis_index("narrow")
@@ -113,11 +116,12 @@
     half_at = pl.multiple_of(par * HEAD, HEAD)
     copies = [
         pltpu.make_async_copy(tok_hbm, x_v, local_sem.at[0]),
-        pltpu.make_async_copy(
-            wqkv_hbm, wqkv_v.at[pl.ds(pl.multiple_of(w * rows, 64), rows)], local_sem.at[1]
-        ),
+        pltpu.make_async_copy(wq_hbm, wqkv_v.at[own_rows, pl.ds(0, q_cols)], local_sem.at[1]),
         pltpu.make_async_copy(cache_hbm, cache_v, local_sem.at[2]),
         pltpu.make_async_copy(cache_hbm.at[0], kvp_v.at[w], local_sem.at[3]),
+        pltpu.make_async_copy(
+            wkv_hbm, wqkv_v.at[own_rows, pl.ds(q_cols, wkv_hbm.shape[1])], local_sem.at[7]
+        ),
     ]
     for copy in copies:
         copy.start()
@@ -179,13 +183,13 @@
         return kvp_v.at[chunk] if part is None else kvp_v.at[chunk, part]
 
     views = [row_view(wqkv_v), prompt_view, row_view(wo_v)]
-    owns = [wqkv_hbm, cache_hbm.at[0], wot_v]
+    owns = [None, cache_hbm.at[0], wot_v]
     started = []
 
     def message(a, kind, chunk, part, to, own=False):
         dst = views[a](chunk, part)
         return pltpu.make_async_remote_copy(
-            src_ref=owns[a] if own else dst,
+            src_ref=owns[a] if own and a > 0 else dst,
             dst_ref=dst,
             send_sem=g_send.at[a, kind],
             recv_sem=g_recv.at[a, kind],
@@ -243,6 +247,8 @@
         ):
             arrived(a, kind, sib(chunk))
 
+    copies[1].wait()
+    copies[4].wait()
     first(0)
     first(1)
 
@@ -351,7 +357,6 @@
     near_x_copy().start()
     fifth(0)
     finish(0)
-    copies[1].wait()
     fourth(1)
     second(2)
     z_copy(2).start()
@@ -540,12 +545,20 @@
         att_v[n, :, pl.ds(pl.multiple_of(h * HEAD, HEAD), HEAD)] = (acc_v[...] / den_v[...]).astype(BF16)
         give(h, 2, 0, 1)
 
+        @pl.when(h > 0)
+        def _():
+            pass_on(h - 1)
+
+        @pl.when(h > 1)
+        def _():
+            pass_further(h - 2)
+
         @pl.when(h == 0)
         def _():
             fourth(2)
             lax.fori_loop(PAIRS // 2, PAIRS, to_partner, 0)
 
-        @pl.when(h == 1)
+        @pl.when(h == 3)
         def _():
             fifth(2)
 
@@ -557,14 +570,6 @@
             lax.fori_loop(0, PAIRS, far_ready, 0)
             to_owners(1)
             own_page(1).start()
-
-        @pl.when(h > 0)
-        def _():
-            pass_on(h - 1)
-
-        @pl.when(h > 1)
-        def _():
-            pass_further(h - 2)
 
         return carry
 
@@ -653,9 +658,8 @@
     page_rows = cache_rows // pages
     half = layers // 2
     cols = q_cols + 2 * channels
-    wqkv = jnp.concatenate([w_query, w_keyval.reshape(rows, 2 * channels)], 1)
-    freq = 1000000.0 ** (-jnp.arange(HEAD // 2, dtype=jnp.float32) * 2.0 / HEAD)
-    freq = jnp.concatenate([freq, freq])[None]
+    freq = 1000000.0 ** (-np.arange(HEAD // 2) * 2.0 / HEAD)
+    freq = jnp.asarray(np.concatenate([freq, freq])[None], jnp.float32)
     any_spec = pl.BlockSpec(memory_space=pl.ANY)
     vmem_spec = pl.BlockSpec(memory_space=pltpu.VMEM)
     smem_spec = pl.BlockSpec(memory_space=pltpu.SMEM)
@@ -668,7 +672,7 @@
             jax.ShapeDtypeStruct((1, half, kinds, WIDE, page_rows, 2 * channels), BF16),
         ),
         in_specs=[
-            any_spec, vmem_spec, any_spec, any_spec, any_spec, vmem_spec,
+            any_spec, vmem_spec, any_spec, any_spec, any_spec, any_spec, vmem_spec,
             smem_spec, smem_spec, smem_spec,
         ],
         out_specs=(vmem_spec, any_spec),
@@ -695,7 +699,7 @@
             pltpu.VMEM((tok_rows, HEAD), F32),
             pltpu.VMEM((tok_rows, HEAD), jnp.int32),
             pltpu.VMEM((tok_rows, q_cols), F32),
-            dma((7,)),
+            dma((8,)),
             dma((3, MESSAGES)),
             dma((3, MESSAGES)),
             dma((2,)),
@@ -717,7 +721,7 @@
             collective_id=0, has_side_effects=True, vmem_limit_bytes=60 * 2**20
         ),
     )(
-        tokens, norm_gain[None], wqkv, w_output.T, cache5, freq,
+        tokens, norm_gain[None], w_query, w_keyval.reshape(rows, 2 * channels), w_output.T, cache5, freq,
         stretch_lengths, stretch_starts, page_route,
     )
     return attn_out, relay

time: 186 us -> 177 us (0.952)
  the two profiles are of different devices: /device:TPU:32 before, /device:TPU:96 now
where the time goes in v5:
time: 177 us
  Pallas kernels  168 us (95%)
  local copies, waits for them, and re-layouts  8.26 us (5%)
    pallas_call x1, Pallas kernels, on_device(): pl.pallas_call(whole_kernel, out_shape=(jax.ShapeDtypeStruct((tok_rows, q...  168 us
    unnamed x3, local copies, waits for them, and re-layouts  8.26 us

profile of v5, /device:TPU:96, one launch (start us, length us, event | category | flops | bytes accessed | tf_op | source)
XLA Modules:
  0.0 177.1 jit_solution(10722979709120160237)
XLA Ops:
  0.6 1.6 copy.14
  2.2 168.2 %shard_map.113 = (bf16[384,640]{1,0:T(8,128)(2,1)}, bf16[1,8,2,16,32,256]{5,4,3,2,1,0:T(8,128)(2,1)}) custom-call(bf16[384,5120]{1,0:T(8,128)(2,1)} %tok_hbm.1, f32[1,5120]{1,0:T(1,128)} %bitcast.11, bf16[320,640]{1,0:T(8,128)(2,1)} %wq_hbm.1, bf16[320,256]{1,0:T(8,128)(2,1)} %bitcast.8, bf16[320,640]{1,0:T(8,128)(2,1)} %bitcast.9, ...), custom_call_target="tpu_custom_call" | custom-call | tf_op jit(solution)/shard_map/pallas_call | solution.py:668
  170.5 1.9 %copy.17 = bf16[384,640]{1,0:T(8,128)(2,1)} copy(bf16[384,640]{1,0:T(8,128)(2,1)} %get-tuple-element.4) | data formatting | bytes 983040
  172.3 4.8 %copy.18 = bf16[1,8,2,16,32,256]{5,4,3,2,1,0:T(8,128)(2,1)} copy(bf16[1,8,2,16,32,256]{5,4,3,2,1,0:T(8,128)(2,1)} %get-tuple-element.5) | data formatting | bytes 8388608

commit v6 on v5

--- a/solution.py
+++ b/solution.py
@@ -558,7 +558,7 @@
             fourth(2)
             lax.fori_loop(PAIRS // 2, PAIRS, to_partner, 0)
 
-        @pl.when(h == 3)
+        @pl.when(h == 2)
         def _():
             fifth(2)
 

time: 177 us -> 179 us (1.011)
  the two profiles are of different devices: /device:TPU:96 before, /device:TPU:32 now
where the time goes in v6:
time: 179 us
  Pallas kernels  170 us (95%)
  local copies, waits for them, and re-layouts  8.26 us (5%)
    pallas_call x1, Pallas kernels, on_device(): pl.pallas_call(whole_kernel, out_shape=(jax.ShapeDtypeStruct((tok_rows, q...  170 us
    unnamed x3, local copies, waits for them, and re-layouts  8.26 us

profile of v6, /device:TPU:32, one launch (start us, length us, event | category | flops | bytes accessed | tf_op | source)
XLA Modules:
  0.0 178.5 jit_solution(11825215170537045112)
XLA Ops:
  0.6 1.6 copy.14
  2.2 169.6 %shard_map.113 = (bf16[384,640]{1,0:T(8,128)(2,1)}, bf16[1,8,2,16,32,256]{5,4,3,2,1,0:T(8,128)(2,1)}) custom-call(bf16[384,5120]{1,0:T(8,128)(2,1)} %tok_hbm.1, f32[1,5120]{1,0:T(1,128)} %bitcast.11, bf16[320,640]{1,0:T(8,128)(2,1)} %wq_hbm.1, bf16[320,256]{1,0:T(8,128)(2,1)} %bitcast.8, bf16[320,640]{1,0:T(8,128)(2,1)} %bitcast.9, ...), custom_call_target="tpu_custom_call" | custom-call | tf_op jit(solution)/shard_map/pallas_call | solution.py:668
  171.9 1.9 %copy.17 = bf16[384,640]{1,0:T(8,128)(2,1)} copy(bf16[384,640]{1,0:T(8,128)(2,1)} %get-tuple-element.4) | data formatting | bytes 983040
  173.7 4.8 %copy.18 = bf16[1,8,2,16,32,256]{5,4,3,2,1,0:T(8,128)(2,1)} copy(bf16[1,8,2,16,32,256]{5,4,3,2,1,0:T(8,128)(2,1)} %get-tuple-element.5) | data formatting | bytes 8388608
